TPU v7x, 128 devices: a whole 4x4x4 slice. The times are simulated.
128 devices in a mesh: sub: 16 (over x, z), crs: 8 (over y, core).
Axes of the slice: x: 4, y: 4, z: 4, core: 2. Of those that a mesh axis runs over, the one named last changes fastest.
Arguments:
- right_side: float32 [64, 2097152], P(None, ('sub', 'crs')), may hold values from -18 to 18
- kappa_sq: float32 [2097152], P(('sub', 'crs')), may hold values from 0.05 to 0.5
- conduct: float32 [2097152], P(('sub', 'crs')), may hold values from 0.1 to 1
- partners: int32 [16384, 4], P(('sub', 'crs')), may hold values from 0 to 16383, as said below
- local_factor: float32 [16384, 128, 128], P(('sub', 'crs')), may hold values from -1 to 3
- restrict_weight: float32 [2097152], P(('sub', 'crs')), may hold values from 0.1 to 0.5
- aggregate: int32 [128, 16384], P(('sub', 'crs')), may hold values from 0 to 511, never falling along the last dimension, each value on 1 to 64 neighbouring positions
- owner: int32 [65536, 1], P(('sub', 'crs')), may hold values from 0 to 15; in each aligned block of 512 rows (0 to 511, 512 to 1023, ...) at most 128 rows name the same one
- owner_coarse_row: int32 [65536], P(('sub', 'crs')), may hold values from 0 to 511
- coarse_factor: float32 [8192, 8192], P('crs', 'sub'), may hold values from -0.0625 to 0.0625
Outputs:
- solution: float32 [64, 2097152], P(None, ('sub', 'crs'))
- residual: float32 [64, 2097152], P(None, ('sub', 'crs'))
Inputs may be any that keep to these rules, and one draw needn't show every extreme that they name: In every slot k the relation is mutual: partners[partners[b, k], k] = b; a block may name itself; every partner lies on its block's subdomain or at most 7 blocks beyond its edge, and slot 0 stays on the subdomain. `aggregate`: each subdomain's row numbers its 512 slots in node order; every slot holds 1 to 64 nodes, and some slot holds exactly 64. Among the 512 slots of one subdomain no owner group is named more than 128 times, a bound that some block reaches.
All inputs are finite; a program needn't handle non-finite values.
Results may differ from a plain program's by a relative error of at most 0.0001.
Values sent between devices are 32-bit elements; how exact they have to be, the bound alone decides.
A program may use at most 256 MiB of HBM per device.

v0:
```python
import jax
import jax.numpy as jnp
from jax import lax
from jax.sharding import PartitionSpec as P

ITERS = 2
HALO_BLK = 7


def extended_2(block, sides, width):
    for axis, dim in sides:
        count = lax.axis_size(axis)
        forward = [(i, i + 1) for i in range(count - 1)]
        backward = [(target, source) for source, target in forward]
        low = lax.ppermute(
            lax.slice_in_dim(block, block.shape[dim] - width, None, axis=dim), axis, forward
        )
        high = lax.ppermute(lax.slice_in_dim(block, 0, width, axis=dim), axis, backward)
        block = jnp.concatenate([low, block, high], axis=dim)
    return block


def per_device(
    right_side,
    kappa_sq,
    conduct,
    partners,
    local_factor,
    restrict_weight,
    aggregate,
    owner,
    owner_coarse_row,
    coarse_factor,
):
    sample_count, node_count = right_side.shape
    block_count = local_factor.shape[0]
    block_width = local_factor.shape[1]
    halo_depth = HALO_BLK
    sub_count = lax.axis_size("sub")
    highest = lax.Precision.HIGHEST
    device = lax.axis_index(("sub", "crs"))
    first_block = device * block_count - halo_depth
    conduct_ext = extended_2(conduct, ((("sub", "crs"), 0),), halo_depth * block_width)
    conduct_ext = conduct_ext.reshape(block_count + 2 * halo_depth, block_width)
    conduct_blocks = conduct.reshape(block_count, block_width)
    kappa_blocks = kappa_sq.reshape(block_count, block_width)
    local_index = partners - first_block
    partner_wt = [0.5 * (conduct_blocks + conduct_ext[local_index[:, k]]) for k in range(4)]
    chain_weight = 0.5 * (conduct_blocks[:, :-1] + conduct_blocks[:, 1:])
    node_slot_table = aggregate[0]
    slot_count = owner.shape[0]
    owner_ids = owner[:, 0]
    coarse_cols = coarse_factor.shape[1]
    coarse_ids = owner_ids * coarse_cols + owner_coarse_row

    def coarse_level(vector_in):
        weighted_values = vector_in * restrict_weight[None, :]
        restriction_tiles = jax.ops.segment_sum(
            weighted_values.T, node_slot_table, num_segments=slot_count, indices_are_sorted=True
        ).T
        dense_part = (
            jnp.zeros((sample_count, coarse_cols * sub_count), jnp.float32)
            .at[:, coarse_ids]
            .add(restriction_tiles)
        )
        partial_value = lax.psum_scatter(dense_part, "sub", scatter_dimension=1, tiled=True)
        coarse_vec = lax.psum(partial_value, "crs")
        halfway_part = lax.dot_general(
            coarse_vec, coarse_factor, (((1,), (1,)), ((), ())), precision=highest
        )
        halfway = lax.psum(halfway_part, "sub")
        lifted_part = jnp.dot(halfway, coarse_factor, precision=highest)
        lifted = lax.psum(lifted_part, "crs")
        lifted_all = lax.all_gather(lifted, "sub", axis=1, tiled=True)
        slot_values = jnp.take(lifted_all, coarse_ids, axis=1)
        return restrict_weight[None, :] * jnp.take(slot_values, node_slot_table, axis=1)

    def precondition(vector_in):
        blocks = vector_in.reshape(sample_count, block_count, block_width)
        halfway = jnp.einsum("sbn,bnm->sbm", blocks, local_factor, precision=highest)
        local_part = jnp.einsum("sbm,bnm->sbn", halfway, local_factor, precision=highest).reshape(
            sample_count, node_count
        )
        return local_part + coarse_level(vector_in)

    def norm_sum(residual, precond):
        return lax.psum(jnp.sum(residual * precond, axis=1), ("sub", "crs"))

    solution = jnp.zeros_like(right_side)
    residual = right_side
    precond = precondition(residual)
    direction = precond
    norm_now = norm_sum(residual, precond)
    for step in range(ITERS):
        extended = extended_2(direction, ((("sub", "crs"), 1),), halo_depth * block_width)
        extended = extended.reshape(sample_count, block_count + 2 * halo_depth, block_width)
        apply_blocks = direction.reshape(sample_count, block_count, block_width)
        result = kappa_blocks * apply_blocks
        for apply_k in range(4):
            partner_vals = jnp.take(extended, local_index[:, apply_k], axis=1)
            result = result + partner_wt[apply_k] * (apply_blocks - partner_vals)
        chain_flux = chain_weight * (apply_blocks[:, :, :-1] - apply_blocks[:, :, 1:])
        result = (
            result
            + jnp.pad(chain_flux, ((0, 0), (0, 0), (0, 1)))
            - jnp.pad(chain_flux, ((0, 0), (0, 0), (1, 0)))
        )
        image = result.reshape(sample_count, node_count)
        curvature = lax.psum(jnp.sum(direction * image, axis=1), ("sub", "crs"))
        step_size = norm_now / curvature
        solution = solution + step_size[:, None] * direction
        residual = residual - step_size[:, None] * image
        if step + 1 < ITERS:
            precond = precondition(residual)
            norm_next = norm_sum(residual, precond)
            direction = precond + (norm_next / norm_now)[:, None] * direction
            norm_now = norm_next
    return (solution, residual)


def solution(mesh):
    return jax.shard_map(
        per_device,
        mesh=mesh,
        in_specs=(
            P(None, ("sub", "crs")),
            P(("sub", "crs")),
            P(("sub", "crs")),
            P(("sub", "crs"), None),
            P(("sub", "crs"), None, None),
            P(("sub", "crs")),
            P(("sub", "crs"), None),
            P(("sub", "crs"), None),
            P(("sub", "crs")),
            P("crs", "sub"),
        ),
        out_specs=(P(None, ("sub", "crs")), P(None, ("sub", "crs"))),
        check_vma=False,
    )
```

profile of v0, /device:TPU:1, one launch (start us, length us, event | category | flops | bytes accessed | tf_op | source)
XLA Modules:
  0.0 1495.6 jit_solution(7455607016218538819)
XLA Ops:
  7.3 7.1 copy.23
  14.4 119.8 %scatter_custom_fusion = f32[512,64]{1,0:T(8,128)S(1)} fusion(s32[16384]{0:T(1024)S(1)} %bitcast.197, f32[64,16384]{0,1:T(8,128)} %copy.23, f32[16384]{0:T(1024)S(1)} %copy-done.6, f32[]{:T(128)} %constant.6.clone.1), kind=kCustom, calls=%fused_computation.68 | custom fusion | flops 2097152 | bytes 4390916 | tf_op jit(solution)/shard_map/scatter-add | solution.py:58
  134.3 4.5 scatter_custom_fusion.1
  138.8 79.5 %reduce-scatter.3.cloned.1.call-done = f32[64,512]{0,1:T(8,128)} async-done(((f32[64,8192]{0,1:T(8,128)}), f32[64,512]{0,1:T(8,128)}) %reduce-scatter.3.cloned.1.call-update) | async-done | bytes 131088 | tf_op jit(solution)/shard_map/reduce_scatter | solution.py:66
  218.4 61.1 %all-reduce.12.cloned.1.call-done = f32[64,512]{0,1:T(8,128)} async-done(((f32[64,512]{0,1:T(8,128)}), f32[64,512]{0,1:T(8,128)}) %all-reduce.12.cloned.1.call-update) | async-done | bytes 131088 | tf_op jit(solution)/shard_map/psum | solution.py:67
  279.5 3.8 fusion.64
  283.4 84.3 %all-reduce.14.cloned.1.call-done = f32[64,1024]{1,0:T(8,128)} async-done(((f32[64,1024]{1,0:T(8,128)}), f32[64,1024]{1,0:T(8,128)}) %all-reduce.14.cloned.1.call-update) | async-done | bytes 262160 | tf_op jit(solution)/shard_map/psum | solution.py:71
  367.7 3.0 fusion.65
  370.8 5.0 collective-permute-start
  375.8 1.9 collective-permute-start.1
  377.7 51.0 %all-reduce.16.cloned.1.call-done = f32[64,512]{1,0:T(8,128)} async-done(((f32[64,512]{1,0:T(8,128)}), f32[64,512]{1,0:T(8,128)}) %all-reduce.16.cloned.1.call-update) | async-done | bytes 131088 | tf_op jit(solution)/shard_map/psum | solution.py:73
  429.5 10.5 fusion.34
  440.0 20.0 %fusion.43 = f32[64,128,128]{2,0,1:T(8,128)} fusion(f32[128,128,128]{2,1,0:T(8,128)} %param.20, f32[128,128,64]{1,2,0:T(8,128)S(1)} %fusion.34), kind=kOutput, calls=%fused_computation.85 | convolution fusion | flops 1610612736 | bytes 16777216 | tf_op jit(solution)/shard_map/sbm,bnm->sbn/dot_general | solution.py:81
  460.0 6.9 copy.31
  469.5 6.7 all-gather.3.cloned.1.call-done
  476.2 3.8 copy.21
  480.0 3.2 gather_fusion.4
  483.4 54.8 %gather_fusion.5 = f32[16384,64]{1,0:T(8,128)} fusion(f32[64,512]{0,1:T(8,128)S(1)} %select_bitcast_fusion.1, s32[16384]{0:T(1024)S(1)} %fusion.56), kind=kCustom, calls=%fused_computation.1.clone | custom fusion | bytes 8454144 | tf_op jit(solution)/shard_map/jit(_take)/gather | solution.py:76
  538.2 6.9 fusion.29
  545.2 4.7 collective-permute-start.2
  549.8 2.1 collective-permute-start.3
  551.9 6.7 fusion.1
  559.6 7.3 pad_maximum_fusion
  567.0 8.0 gather_fusion.6
  574.9 8.0 gather_fusion.7
  582.9 8.0 gather_fusion.8
  591.0 8.0 gather_fusion.9
  599.0 20.1 %fusion.22 = f32[64,128,128]{0,2,1:T(8,128)S(1)} fusion(f32[64,128,128]{0,2,1:T(8,128)} %bitcast.182, f32[128,64,128]{1,2,0:T(8,128)} %gather_fusion.9, f32[128,64,128]{1,2,0:T(8,128)} %gather_fusion.8, f32[128,64,128]{1,2,0:T(8,128)} %gather_fusion.7, f32[128,64,128]{1,2,0:T(8,128)} %gather_fusion.6, f32[64,128,127]{0,2,1:T(8,128)} %fusion.1, ...), kind=kLoop, calls=%fused_computation.56 | loop fusion | flops 19922944 | bytes 29655552 | tf_op jit(solution)/shard_map/sub | solution.py:104
  619.1 10.0 fusion.17
  629.1 68.1 %all-reduce.4 = (f32[64]{0:T(128)S(1)}, f32[64]{0:T(128)S(1)}) all-reduce(f32[64]{0:T(128)S(1)} %get-tuple-element.10, f32[64]{0:T(128)S(1)} %get-tuple-element.9), channel_id=1, replica_groups=mesh['sub'=16,'crs'=8] {'sub','crs'}, use_global_device_ids=true, to_apply=%region_7.10 | all-reduce | flops 128 | bytes 1024 | tf_op jit(solution)/shard_map/psum | solution.py:87
  697.2 9.8 fusion.18
  707.0 119.8 %scatter_custom_fusion.2 = f32[512,64]{1,0:T(8,128)S(1)} fusion(s32[16384]{0:T(1024)S(1)} %bitcast.200, f32[64,16384]{0,1:T(8,128)} %fusion.18, f32[16384]{0:T(1024)S(1)} %copy-done.6, f32[]{:T(128)} %constant.6.clone.1), kind=kCustom, calls=%fused_computation.46 | custom fusion | flops 2097152 | bytes 4390916 | tf_op jit(solution)/shard_map/scatter-add | solution.py:58
  826.8 4.5 scatter_custom_fusion.3
  831.4 74.1 %reduce-scatter.5.cloned.1.call-done = f32[64,512]{0,1:T(8,128)} async-done(((f32[64,8192]{0,1:T(8,128)}), f32[64,512]{0,1:T(8,128)}) %reduce-scatter.5.cloned.1.call-update) | async-done | bytes 131088 | tf_op jit(solution)/shard_map/reduce_scatter | solution.py:66
  905.5 61.0 %all-reduce.18.cloned.1.call-done = f32[64,512]{0,1:T(8,128)} async-done(((f32[64,512]{0,1:T(8,128)}), f32[64,512]{0,1:T(8,128)}) %all-reduce.18.cloned.1.call-update) | async-done | bytes 131088 | tf_op jit(solution)/shard_map/psum | solution.py:67
  966.5 3.8 fusion.67
  970.5 84.3 %all-reduce.20.cloned.1.call-done = f32[64,1024]{1,0:T(8,128)} async-done(((f32[64,1024]{1,0:T(8,128)}), f32[64,1024]{1,0:T(8,128)}) %all-reduce.20.cloned.1.call-update) | async-done | bytes 262160 | tf_op jit(solution)/shard_map/psum | solution.py:71
  1054.8 3.0 fusion.68
  1058.3 57.5 %all-reduce.22.cloned.1.call-done = f32[64,512]{1,0:T(8,128)} async-done(((f32[64,512]{1,0:T(8,128)}), f32[64,512]{1,0:T(8,128)}) %all-reduce.22.cloned.1.call-update) | async-done | bytes 131088 | tf_op jit(solution)/shard_map/psum | solution.py:73
  1115.8 17.4 %fusion.66 = f32[128,64,128]{2,1,0:T(8,128)S(1)} fusion(f32[64,128,128]{0,2,1:T(8,128)} %bitcast.185, f32[128,128,128]{2,1,0:T(8,128)} %param.20), kind=kOutput, calls=%fused_computation.139 | convolution fusion | flops 1610612736 | bytes 16777216 | tf_op jit(solution)/shard_map/sbn,bnm->sbm/dot_general | solution.py:80
  1133.1 19.8 %fusion.46 = f32[64,128,128]{2,0,1:T(8,128)} fusion(f32[128,128,128]{2,1,0:T(8,128)} %param.20, f32[128,64,128]{2,1,0:T(8,128)S(1)} %fusion.66), kind=kOutput, calls=%fused_computation.86 | convolution fusion | flops 1610612736 | bytes 16777216 | tf_op jit(solution)/shard_map/sbm,bnm->sbn/dot_general | solution.py:81
  1153.0 6.9 copy.32
  1159.9 3.2 all-gather.5.cloned.1.call-done
  1163.1 3.8 copy.26
  1167.0 3.2 gather_fusion.10
  1170.4 54.8 %gather_fusion.11 = f32[16384,64]{1,0:T(8,128)} fusion(f32[64,512]{0,1:T(8,128)S(1)} %select_bitcast_fusion, s32[16384]{0:T(1024)S(1)} %fusion.56), kind=kCustom, calls=%fused_computation.4.clone | custom fusion | bytes 8454144 | tf_op jit(solution)/shard_map/jit(_take)/gather | solution.py:76
  1225.1 8.7 multiply_reduce_fusion
  1233.9 65.5 %psum.78 = f32[64]{0:T(128)S(1)} all-reduce(f32[64]{0:T(128)S(1)} %multiply_reduce_fusion), channel_id=1, replica_groups=mesh['sub'=16,'crs'=8] {'sub','crs'}, use_global_device_ids=true, to_apply=%region_17.21 | all-reduce | flops 64 | bytes 512 | tf_op jit(solution)/shard_map/psum | solution.py:87
  1299.4 8.8 multiply_add_fusion.1
  1308.3 2.2 collective-permute-start.4
  1310.5 2.1 collective-permute-start.5
  1312.6 6.8 fusion
  1320.3 7.3 pad_maximum_fusion.1
  1327.6 8.0 gather_fusion.12
  1335.7 8.0 gather_fusion.13
  1343.6 8.0 gather_fusion.14
  1351.6 8.0 gather_fusion.15
  1359.6 20.5 %fusion.7 = f32[64,128,128]{0,2,1:T(8,128)S(1)} fusion(f32[64,128,128]{0,2,1:T(8,128)} %bitcast.184, f32[128,64,128]{1,2,0:T(8,128)} %gather_fusion.15, f32[128,64,128]{1,2,0:T(8,128)} %gather_fusion.14, f32[128,64,128]{1,2,0:T(8,128)} %gather_fusion.13, f32[128,64,128]{1,2,0:T(8,128)} %gather_fusion.12, f32[64,128,127]{0,2,1:T(8,128)} %fusion, ...), kind=kLoop, calls=%fused_computation.34 | loop fusion | flops 19922944 | bytes 29655552 | tf_op jit(solution)/shard_map/sub | solution.py:104
  1380.2 3.2 copy-done.4
  1383.4 4.6 fusion.2
  1388.0 69.2 %psum.79 = f32[64]{0:T(128)S(1)} all-reduce(f32[64]{0:T(128)S(1)} %fusion.2), channel_id=1, replica_groups=mesh['sub'=16,'crs'=8] {'sub','crs'}, use_global_device_ids=true, to_apply=%region_19.23 | all-reduce | flops 64 | bytes 512 | tf_op jit(solution)/shard_map/psum | solution.py:109
  1457.2 17.6 %fusion.3 = (f32[64,16384]{0,1:T(8,128)}, f32[64,16384]{0,1:T(8,128)}) fusion(f32[64,16384]{0,1:T(8,128)} %fusion.18, f32[64,128,128]{0,2,1:T(8,128)} %copy-done.4, f32[64]{0:T(128)S(1)} %div.11, f32[64,16384]{0,1:T(8,128)} %copy-done.3, f32[64,16384]{0,1:T(8,128)} %copy-done.2, f32[64]{0:T(128)S(1)} %div.9), kind=kLoop, calls=%fused_computation.29 | loop fusion | flops 5242880 | bytes 25166336 | tf_op jit(solution)/shard_map/sub | solution.py:112
  1474.9 6.9 copy.28
  1481.8 6.8 copy.29
  (78 shorter events, 6.5 us)
Async XLA Ops:
  7.2 272.3 %copy-start = (f32[1024,512]{1,0:T(8,128)S(1)}, f32[1024,512]{1,0:T(8,128)}, u32[]{:S(2)}) copy-start(f32[1024,512]{1,0:T(8,128)} %param.25) | copy-start | bytes 6291460
  7.2 7.2 copy-start.10
  7.2 7.2 copy-start.11
  7.2 7.2 copy-start.9
  7.2 7.2 copy-start.6
  7.2 211.1 %reduce-scatter.3.cloned.1.call-start = ((), (), s32[]{:S(2)}) async-start(), calls=%async_computation.2 | async-start | bytes 4456448 | tf_op jit(solution)/shard_map/reduce_scatter | solution.py:66
  134.2 236.6 %copy-start.7 = (f32[16384]{0:T(1024)S(1)}, f32[16384]{0:T(1024)}, u32[]{:S(2)}) copy-start(f32[16384]{0:T(1024)} %param.18) | copy-start | bytes 196612
  134.2 295.0 %copy-start.12 = (s32[128,4]{0,1:T(4,128)S(1)}, s32[128,4]{0,1:T(4,128)}, u32[]{:S(2)}) copy-start(s32[128,4]{0,1:T(4,128)} %param.19) | copy-start | bytes 6148
  138.8 140.7 %all-reduce.12.cloned.1.call-start = ((), (), s32[]{:S(2)}) async-start(), calls=%async_computation.3 | async-start | bytes 524288 | tf_op jit(solution)/shard_map/psum | solution.py:67
  218.3 149.4 %all-reduce.14.cloned.1.call-start = ((), (), s32[]{:S(2)}) async-start(), calls=%async_computation.4 | async-start | bytes 524288 | tf_op jit(solution)/shard_map/psum | solution.py:71
  283.3 145.4 %all-reduce.16.cloned.1.call-start = ((), (), s32[]{:S(2)}) async-start(), calls=%async_computation.5 | async-start | bytes 262144 | tf_op jit(solution)/shard_map/psum | solution.py:73
  370.7 105.4 %all-gather.3.cloned.1.call-start = ((), (), s32[]{:S(2)}) async-start(), calls=%async_computation.6 | async-start | bytes 2228224 | tf_op jit(solution)/shard_map/all_gather | solution.py:74
  370.8 96.1 %collective-permute-start = (f32[896]{0:T(1024)S(1)}, f32[896]{0:T(1024)S(1)}, u32[]{:S(2)}, u32[]{:S(2)}) collective-permute-start(f32[896]{0:T(1024)S(1)} %get-tuple-element.31), channel_id=1, source_target_pairs={{0,1},{1,2},{2,3},{3,4},{4,5},{5,6},{6,7},{7,8},{8,9},{9,10},{10,1... | collective-permute-start | bytes 10760 | tf_op jit(solution)/shard_map/ppermute | solution.py:15
  375.8 91.1 %collective-permute-start.1 = (f32[896]{0:T(1024)S(1)}, f32[896]{0:T(1024)S(1)}, u32[]{:S(2)}, u32[]{:S(2)}) collective-permute-start(f32[896]{0:T(1024)S(1)} %get-tuple-element.32), channel_id=1, source_target_pairs={{1,0},{2,1},{3,2},{4,3},{5,4},{6,5},{7,6},{8,7},{9,8},{10,9},{11,1... | collective-permute-start | bytes 10760 | tf_op jit(solution)/shard_map/ppermute | solution.py:18
  428.7 476.7 %reduce-scatter.5.cloned.1.call-start = ((), (), s32[]{:S(2)}) async-start(), calls=%async_computation.7 | async-start | bytes 4456448 | tf_op jit(solution)/shard_map/reduce_scatter | solution.py:66
  545.1 14.5 copy-start.2
  545.2 13.5 collective-permute-start.2
  549.8 9.8 collective-permute-start.3
  582.9 16.0 %copy-start.8 = (f32[16384]{0:T(1024)S(1)}, f32[16384]{0:T(1024)}, u32[]{:S(2)}) copy-start(f32[16384]{0:T(1024)} %param.17) | copy-start | bytes 196612
  619.1 10.0 copy-start.5
  831.3 135.2 %all-reduce.18.cloned.1.call-start = ((), (), s32[]{:S(2)}) async-start(), calls=%async_computation.8 | async-start | bytes 524288 | tf_op jit(solution)/shard_map/psum | solution.py:67
  905.5 149.3 %all-reduce.20.cloned.1.call-start = ((), (), s32[]{:S(2)}) async-start(), calls=%async_computation.9 | async-start | bytes 524288 | tf_op jit(solution)/shard_map/psum | solution.py:71
  970.4 145.3 %all-reduce.22.cloned.1.call-start = ((), (), s32[]{:S(2)}) async-start(), calls=%async_computation.10 | async-start | bytes 262144 | tf_op jit(solution)/shard_map/psum | solution.py:73
  1057.8 105.3 %all-gather.5.cloned.1.call-start = ((), (), s32[]{:S(2)}) async-start(), calls=%async_computation.11 | async-start | bytes 2228224 | tf_op jit(solution)/shard_map/all_gather | solution.py:74
  1308.2 12.1 copy-start.3
  1308.3 11.2 collective-permute-start.4
  1310.5 9.8 collective-permute-start.5
  1380.1 3.2 copy-start.4
  1474.9 13.7 copy-start.1
Sparse Core Ops, SparseCore 0:
  138.9 79.3 reduce-scatter.2
  220.7 58.6 all-reduce.11
  283.4 84.2 all-reduce.13
  370.9 57.7 all-reduce.15
  430.7 45.3 all-gather.2
  831.4 73.9 reduce-scatter.4
  907.9 58.6 all-reduce.17
  970.5 84.2 all-reduce.19
  1057.9 57.7 all-reduce.21
  1117.8 45.3 all-gather.4
where the time goes:
time: 1500 us
  waiting for transfers between devices  565 us (38%)
  other arithmetic  384 us (26%)
  local copies, waits for them, and re-layouts  228 us (15%)
  blocking collectives  203 us (14%)
  matrix products  81.3 us (5%)
  starting transfers between devices  19.3 us (1%)
    scatter-add x2, other arithmetic, coarse_level(): jax.ops.segment_sum(weighted_values.T, node_slot_table, num_segments=slot...  240 us
    psum x2, waiting for transfers between devices, coarse_level(): halfway = lax.psum(halfway_part, 'sub')  169 us
    reduce_scatter x2, waiting for transfers between devices, coarse_level(): lax.psum_scatter(dense_part, 'sub', scatter_dimension=1, tiled=True)  154 us
    psum x2, blocking collectives, norm_sum(): return lax.psum(jnp.sum(residual * precond, axis=1), ('sub', 'crs'))  134 us
    psum x2, waiting for transfers between devices, coarse_level(): coarse_vec = lax.psum(partial_value, 'crs')  122 us
    gather x2, local copies, waits for them, and re-layouts, coarse_level(): jnp.take(slot_values, node_slot_table, axis=1)  110 us
    psum x2, waiting for transfers between devices, coarse_level(): lifted = lax.psum(lifted_part, 'crs')  108 us
    psum x1, blocking collectives, per_device(): curvature = lax.psum(jnp.sum(direction * image, axis=1), ('sub', 'crs'))  69.2 us
  transfers between devices with their start and end apart: 16, of which 12 were waited for; matrix products, arithmetic and copies ran while one was open for 7% of the time, Pallas kernels for 0%

commit v1 on v0

v1 whole, which is shorter than its diff:
```python
import functools

import jax
import jax.numpy as jnp
from jax import lax
from jax.experimental import pallas as pl
from jax.experimental.pallas import tpu as pltpu
from jax.sharding import PartitionSpec as P

MESH = pl.DeviceIdType.MESH
F32 = jnp.float32
BF16 = jnp.bfloat16
HALO = 7
BS = 128
SMP = 64
LIMIT = 128


def split(x):
    high = x.astype(BF16)
    return high, (x - high.astype(F32)).astype(BF16)


def dot(a, b):
    return lax.dot_general(a, b, (((1,), (0,)), ((), ())), preferred_element_type=F32)


def dot_t(a, b):
    return lax.dot_general(a, b, (((1,), (1,)), ((), ())), preferred_element_type=F32)


def stacked(x):
    return jnp.concatenate(split(x), axis=0)


def folded(y):
    half = y.shape[0] // 2
    return y[:half] + y[half:]


def one_hot(mask):
    return jnp.where(mask, 1.0, 0.0).astype(BF16)


def apply_kernel(
    n_sub,
    n_crs,
    src_hbm,
    factor_hbm,
    coarse_hbm,
    weight_ref,
    kappa_ref,
    cond_ref,
    slot_ref,
    owner_ref,
    row_ref,
    partner_ref,
    z_hbm,
    q_hbm,
    dots_ref,
    src_v,
    factor_v,
    coarse_v,
    ext_v,
    cond_v,
    q_v,
    acc_v,
    place_v,
    scatter_v,
    index_send,
    index_recv,
    slot_send,
    slot_recv,
    back_send,
    back_recv,
    cpart,
    crecv,
    cfull,
    ipart,
    irecv,
    ifull,
    lpart,
    lrecv,
    lfull,
    slot_v,
    load_sem,
    store_sem,
    sub_send,
    sub_recv,
    crs_send,
    crs_recv,
    halo_send,
    halo_recv,
):
    sub = lax.axis_index("sub")
    crs = lax.axis_index("crs")
    me = sub * n_crs + crs
    total = n_sub * n_crs
    right = lax.rem(me + 1, total)
    left = lax.rem(me + total - 1, total)
    nodes = src_v.shape[1]
    blocks = nodes // BS
    slots = owner_ref.shape[1]
    halo = HALO * BS

    def sub_peer(j):
        return lax.rem(sub + j, n_sub)

    def sub_from(j):
        return lax.rem(sub + n_sub - j, n_sub)

    def crs_peer(j):
        return lax.rem(crs + j, n_crs)

    def crs_from(j):
        return lax.rem(crs + n_crs - j, n_crs)

    def at_device(d):
        return (d // n_crs, lax.rem(d, n_crs))

    def sub_copy(phase, j, source, target):
        return pltpu.make_async_remote_copy(
            src_ref=source,
            dst_ref=target,
            send_sem=sub_send.at[phase, j],
            recv_sem=sub_recv.at[phase, j],
            device_id=(sub_peer(j), crs),
            device_id_type=MESH,
        )

    def crs_copy(phase, j, source, target):
        return pltpu.make_async_remote_copy(
            src_ref=source,
            dst_ref=target,
            send_sem=crs_send.at[phase, j],
            recv_sem=crs_recv.at[phase, j],
            device_id=(sub, crs_peer(j)),
            device_id_type=MESH,
        )

    def lanes(ref, i):
        return ref.at[:, pl.ds(pl.multiple_of(i * LIMIT, LIMIT), LIMIT)]

    def start_all(count, copy):
        @pl.loop(1, count)
        def _(j):
            copy(j).start()

    def wait_all(count, copy):
        @pl.loop(1, count)
        def _(j):
            copy(j).wait()

    loads = [
        pltpu.make_async_copy(src_hbm, src_v, load_sem.at[0]),
        pltpu.make_async_copy(factor_hbm, factor_v, load_sem.at[1]),
        pltpu.make_async_copy(coarse_hbm, coarse_v, load_sem.at[2]),
    ]
    for load in loads:
        load.start()

    barrier = pltpu.get_barrier_semaphore()

    @pl.loop(1, n_sub)
    def _(j):
        pl.semaphore_signal(barrier, inc=1, device_id=(sub_peer(j), crs), device_id_type=MESH)

    @pl.loop(1, n_crs)
    def _(j):
        pl.semaphore_signal(barrier, inc=1, device_id=(sub, crs_peer(j)), device_id_type=MESH)

    pl.semaphore_signal(barrier, inc=1, device_id=at_device(left), device_id_type=MESH)
    pl.semaphore_signal(barrier, inc=1, device_id=at_device(right), device_id_type=MESH)

    owner_row = owner_ref[...]
    group = lax.broadcasted_iota(jnp.int32, (n_sub, slots), 0)
    members = jnp.where(owner_row == group, 1.0, 0.0)
    before = one_hot(
        lax.broadcasted_iota(jnp.int32, (slots, slots), 0)
        < lax.broadcasted_iota(jnp.int32, (slots, slots), 1)
    )
    ahead = dot(members.astype(BF16), before)
    rank = jnp.sum(members * ahead, axis=0, keepdims=True)
    place = owner_row * LIMIT + rank.astype(jnp.int32)
    row_one = stacked(jnp.broadcast_to((row_ref[...] + 1).astype(F32), (8, slots)))

    @pl.loop(0, n_sub)
    def _(i):
        start = pl.multiple_of(i * LIMIT, LIMIT)
        hot = one_hot(lax.broadcasted_iota(jnp.int32, (LIMIT, slots), 0) + start == place)
        place_v[pl.ds(start, LIMIT), :] = hot
        index_send[i] = folded(dot_t(row_one, hot)) - 1.0

    cond_v[:, pl.ds(halo, nodes)] = cond_ref[...]
    index_recv[sub] = index_send[sub]

    pl.semaphore_wait(barrier, n_sub + n_crs)

    def index_copy(j):
        return sub_copy(0, j, index_send.at[sub_peer(j)], index_recv.at[sub])

    def index_wait(j):
        return sub_copy(0, j, index_send.at[sub_peer(j)], index_recv.at[sub_from(j)])

    start_all(n_sub, index_copy)

    def halo_copies(buffer, phase):
        up = pltpu.make_async_remote_copy(
            src_ref=buffer.at[:, pl.ds(nodes, halo)],
            dst_ref=buffer.at[:, pl.ds(0, halo)],
            send_sem=halo_send.at[phase],
            recv_sem=halo_recv.at[phase],
            device_id=at_device(right),
            device_id_type=MESH,
        )
        down = pltpu.make_async_remote_copy(
            src_ref=buffer.at[:, pl.ds(halo, halo)],
            dst_ref=buffer.at[:, pl.ds(halo + nodes, halo)],
            send_sem=halo_send.at[phase + 1],
            recv_sem=halo_recv.at[phase + 1],
            device_id=at_device(left),
            device_id_type=MESH,
        )
        return up, down

    cond_copies = halo_copies(cond_v, 0)
    for copy in cond_copies:
        copy.start()

    loads[0].wait()
    chunk = 1024
    acc_v[...] = jnp.zeros_like(acc_v)

    @pl.loop(0, nodes // chunk)
    def _(i):
        span = pl.ds(pl.multiple_of(i * chunk, chunk), chunk)
        weighted = src_v[:, span] * weight_ref[:, span]
        hot = one_hot(lax.broadcasted_iota(jnp.int32, (slots, chunk), 0) == slot_ref[:, span])
        acc_v[...] += dot_t(stacked(weighted), hot)

    tiles = stacked(folded(acc_v[...]))
    for i in range(0, n_sub, 2):
        slot_send[:, i * LIMIT : (i + 2) * LIMIT] = folded(
            dot_t(tiles, place_v[i * LIMIT : (i + 2) * LIMIT, :])
        )

    def slot_copy(j):
        return sub_copy(1, j, lanes(slot_send, sub_peer(j)), lanes(slot_recv, sub))

    def slot_wait(j):
        return sub_copy(1, j, lanes(slot_send, sub_peer(j)), lanes(slot_recv, sub_from(j)))

    start_all(n_sub, slot_copy)
    own = pl.ds(pl.multiple_of(sub * LIMIT, LIMIT), LIMIT)
    slot_recv[:, own] = slot_send[:, own]

    def local(first, last):
        @pl.loop(first // 4, last // 4)
        def _(g):
            for k in range(4):
                b = g * 4 + k
                at = pl.multiple_of(b * BS, BS)
                values = stacked(src_v[:, pl.ds(at, BS)])
                high, low = split(factor_v[b])
                half = folded(dot(values, high)) + dot(values[:SMP], low)
                half = stacked(half)
                ext_v[:, pl.ds(pl.multiple_of(at + halo, BS), BS)] = folded(
                    dot_t(half, high)
                ) + dot_t(half[:SMP], low)

    loads[1].wait()
    local(0, 32)

    wait_all(n_sub, index_wait)

    @pl.loop(0, n_sub)
    def _(i):
        index = index_recv[i][0:1, :].astype(jnp.int32)
        rows = scatter_v.shape[0]
        span = pl.ds(pl.multiple_of(i * LIMIT, LIMIT), LIMIT)
        scatter_v[:, span] = one_hot(lax.broadcasted_iota(jnp.int32, (rows, LIMIT), 0) == index)

    wait_all(n_sub, slot_wait)
    coarse_part = folded(dot_t(stacked(slot_recv[...]), scatter_v[...]))
    cpart[...] = coarse_part.reshape(cpart.shape)

    def reduce_sub(phase, part, recv, full, gap):
        def out(j):
            return sub_copy(phase, j, part.at[sub_peer(j)], recv.at[sub])

        def come(j):
            return sub_copy(phase, j, part.at[sub_peer(j)], recv.at[sub_from(j)])

        def share(j):
            return sub_copy(phase + 1, j, full.at[sub], full.at[sub])

        def shared(j):
            return sub_copy(phase + 1, j, full.at[sub], full.at[sub_from(j)])

        start_all(n_sub, out)
        recv[sub] = part[sub]
        local(gap, gap + 16)
        wait_all(n_sub, come)
        full[sub] = jnp.sum(recv[...], axis=0)
        start_all(n_sub, share)
        local(gap + 16, gap + 32)
        wait_all(n_sub, shared)

    def reduce_crs(phase, part, recv, full, gap):
        def out(j):
            return crs_copy(phase, j, part.at[crs_peer(j)], recv.at[crs])

        def come(j):
            return crs_copy(phase, j, part.at[crs_peer(j)], recv.at[crs_from(j)])

        def share(j):
            return crs_copy(phase + 1, j, full.at[crs], full.at[crs])

        def shared(j):
            return crs_copy(phase + 1, j, full.at[crs], full.at[crs_from(j)])

        start_all(n_crs, out)
        recv[crs] = part[crs]
        local(gap, gap + 16)
        wait_all(n_crs, come)
        full[crs] = jnp.sum(recv[...], axis=0)
        start_all(n_crs, share)
        local(gap + 16, gap + 32)
        wait_all(n_crs, shared)

    reduce_crs(0, cpart, crecv, cfull, 32)
    loads[2].wait()
    coarse = stacked(cfull[...].reshape(SMP, -1))
    half_rows = coarse_v.shape[0] // 2
    for h in range(2):
        high, low = split(coarse_v[h * half_rows : (h + 1) * half_rows, :])
        inner = folded(dot_t(coarse, high)) + dot_t(coarse[:SMP], low)
        ipart[h * 8 : (h + 1) * 8] = inner.reshape(8, 8, half_rows)

    reduce_sub(2, ipart, irecv, ifull, 64)
    lifted = jnp.zeros((SMP, coarse_v.shape[1]), F32)
    for h in range(2):
        high, low = split(coarse_v[h * half_rows : (h + 1) * half_rows, :])
        inner = stacked(ifull[h * 8 : (h + 1) * 8].reshape(SMP, half_rows))
        lifted = lifted + folded(dot(inner, high)) + dot(inner[:SMP], low)
    lpart[...] = lifted.reshape(lpart.shape)

    reduce_crs(2, lpart, lrecv, lfull, 96)
    lifted = stacked(lfull[...].reshape(SMP, -1))
    for i in range(0, n_sub, 2):
        back_send[:, i * LIMIT : (i + 2) * LIMIT] = folded(
            dot(lifted, scatter_v[:, i * LIMIT : (i + 2) * LIMIT])
        )

    def back_copy(j):
        return sub_copy(4, j, lanes(back_send, sub_peer(j)), lanes(back_recv, sub))

    def back_wait(j):
        return sub_copy(4, j, lanes(back_send, sub_peer(j)), lanes(back_recv, sub_from(j)))

    start_all(n_sub, back_copy)
    back_recv[:, own] = back_send[:, own]
    wait_all(n_sub, back_wait)
    slot_v[...] = stacked(folded(dot(stacked(back_recv[...]), place_v[...])))

    dots_ref[...] = jnp.zeros_like(dots_ref)

    def lift(i):
        at = pl.multiple_of(i * chunk, chunk)
        span = pl.ds(at, chunk)
        hot = one_hot(lax.broadcasted_iota(jnp.int32, (slots, chunk), 0) == slot_ref[:, span])
        inside = pl.ds(pl.multiple_of(at + halo, BS), chunk)
        z = ext_v[:, inside] + weight_ref[:, span] * folded(dot(slot_v[...], hot))
        ext_v[:, inside] = z
        product = z * src_v[:, span]
        total = product[:, :BS]
        for k in range(1, chunk // BS):
            total = total + product[:, k * BS : (k + 1) * BS]
        dots_ref[0] += total

    chunks = nodes // chunk

    @pl.loop(0, 2)
    def _(i):
        lift(i * (chunks - 1))

    halo_now = halo_copies(ext_v, 2)
    for copy in halo_now:
        copy.start()

    @pl.loop(1, chunks - 1)
    def _(i):
        lift(i)

    store_z = pltpu.make_async_copy(ext_v.at[:, pl.ds(halo, nodes)], z_hbm, store_sem.at[0])
    store_z.start()
    for copy in cond_copies:
        copy.wait()
    for copy in halo_now:
        copy.wait()

    lane = lax.broadcasted_iota(jnp.int32, (1, BS), 1)

    def operator(b):
        at = pl.multiple_of(b * BS, BS)
        inside = pl.ds(pl.multiple_of(at + halo, BS), BS)
        v = ext_v[:, inside]
        cond = cond_v[:, inside]
        diagonal = kappa_ref[:, pl.ds(at, BS)]
        up = jnp.where(lane < BS - 1, 0.5 * (cond + pltpu.roll(cond, BS - 1, 1)), 0.0)
        down = jnp.where(lane > 0, 0.5 * (cond + pltpu.roll(cond, 1, 1)), 0.0)
        diagonal = diagonal + up + down
        taken = up * pltpu.roll(v, BS - 1, 1) + down * pltpu.roll(v, 1, 1)
        for k in range(4):
            other = pl.ds(partner_ref[b * 4 + k] * BS, BS)
            weight = 0.5 * (cond + cond_v[:, other])
            diagonal = diagonal + weight
            taken = taken + weight * ext_v[:, other]
        image = diagonal * v - taken
        q_v[:, pl.ds(at, BS)] = image
        dots_ref[1] += v * image

    @pl.loop(0, blocks // 2)
    def _(g):
        operator(g * 2)
        operator(g * 2 + 1)

    store_q = pltpu.make_async_copy(q_v, q_hbm, store_sem.at[1])
    store_q.start()
    store_z.wait()
    store_q.wait()


def apply_call(n_sub, n_crs, src, factor, coarse_factor, weight, kappa, cond, slot, owner, row, partner):
    nodes = src.shape[1]
    blocks = factor.shape[0]
    slots = owner.shape[1]
    rows, cols = coarse_factor.shape
    halo = HALO * BS
    vmem = pl.BlockSpec(memory_space=pltpu.VMEM)
    anywhere = pl.BlockSpec(memory_space=pl.ANY)
    wide = n_sub * LIMIT
    field = jax.ShapeDtypeStruct(src.shape, F32)
    return pl.pallas_call(
        functools.partial(apply_kernel, n_sub, n_crs),
        out_shape=(field, field, jax.ShapeDtypeStruct((2, SMP, BS), F32)),
        in_specs=[anywhere] * 3 + [vmem] * 6 + [pl.BlockSpec(memory_space=pltpu.SMEM)],
        out_specs=(anywhere, anywhere, vmem),
        scratch_shapes=[
            pltpu.VMEM((SMP, nodes), F32),
            pltpu.VMEM((blocks, BS, BS), F32),
            pltpu.VMEM((rows, cols), F32),
            pltpu.VMEM((SMP, nodes + 2 * halo), F32),
            pltpu.VMEM((1, nodes + 2 * halo), F32),
            pltpu.VMEM((SMP, nodes), F32),
            pltpu.VMEM((2 * SMP, slots), F32),
            pltpu.VMEM((wide, slots), BF16),
            pltpu.VMEM((cols, wide), BF16),
            pltpu.VMEM((n_sub, 8, LIMIT), F32),
            pltpu.VMEM((n_sub, 8, LIMIT), F32),
            pltpu.VMEM((SMP, wide), F32),
            pltpu.VMEM((SMP, wide), F32),
            pltpu.VMEM((SMP, wide), F32),
            pltpu.VMEM((SMP, wide), F32),
            pltpu.VMEM((n_crs, 8, cols), F32),
            pltpu.VMEM((n_crs, 8, cols), F32),
            pltpu.VMEM((n_crs, 8, cols), F32),
            pltpu.VMEM((n_sub, 8, rows // 2), F32),
            pltpu.VMEM((n_sub, 8, rows // 2), F32),
            pltpu.VMEM((n_sub, 8, rows // 2), F32),
            pltpu.VMEM((n_crs, 8, cols), F32),
            pltpu.VMEM((n_crs, 8, cols), F32),
            pltpu.VMEM((n_crs, 8, cols), F32),
            pltpu.VMEM((2 * SMP, slots), BF16),
            pltpu.SemaphoreType.DMA((3,)),
            pltpu.SemaphoreType.DMA((2,)),
            pltpu.SemaphoreType.DMA((5, n_sub)),
            pltpu.SemaphoreType.DMA((5, n_sub)),
            pltpu.SemaphoreType.DMA((4, n_crs)),
            pltpu.SemaphoreType.DMA((4, n_crs)),
            pltpu.SemaphoreType.DMA((4,)),
            pltpu.SemaphoreType.DMA((4,)),
        ],
        compiler_params=pltpu.CompilerParams(
            collective_id=0, has_side_effects=True, vmem_limit_bytes=52 * 1024 * 1024
        ),
    )(src, factor, coarse_factor, weight, kappa, cond, slot, owner, row, partner)


def scalar_kernel(n_sub, n_crs, first_ref, second_ref, out_ref, mine, crs_in, part, sub_in, crs_send, crs_recv, sub_send, sub_recv):
    sub = lax.axis_index("sub")
    crs = lax.axis_index("crs")

    def sub_peer(j):
        return lax.rem(sub + j, n_sub)

    def crs_peer(j):
        return lax.rem(crs + j, n_crs)

    barrier = pltpu.get_barrier_semaphore()

    @pl.loop(1, n_sub)
    def _(j):
        pl.semaphore_signal(barrier, inc=1, device_id=(sub_peer(j), crs), device_id_type=MESH)

    @pl.loop(1, n_crs)
    def _(j):
        pl.semaphore_signal(barrier, inc=1, device_id=(sub, crs_peer(j)), device_id_type=MESH)

    kind = lax.broadcasted_iota(jnp.int32, (8, SMP), 0)
    packed = jnp.zeros((8, SMP), F32)
    ones = jnp.ones((8, BS), F32)
    for i in range(4):
        values = (first_ref if i < 2 else second_ref)[i % 2]
        sums = lax.dot_general(
            ones,
            values,
            (((1,), (1,)), ((), ())),
            precision=lax.Precision.HIGHEST,
            preferred_element_type=F32,
        )
        packed = jnp.where(kind == i, sums, packed)
    mine[:, :SMP] = packed
    mine[:, SMP:] = jnp.zeros((8, BS - SMP), F32)
    pl.semaphore_wait(barrier, n_sub + n_crs - 2)

    def crs_copy(j, slot):
        return pltpu.make_async_remote_copy(
            src_ref=mine,
            dst_ref=crs_in.at[slot],
            send_sem=crs_send.at[j],
            recv_sem=crs_recv.at[j],
            device_id=(sub, crs_peer(j)),
            device_id_type=MESH,
        )

    def sub_copy(j, slot):
        return pltpu.make_async_remote_copy(
            src_ref=part,
            dst_ref=sub_in.at[slot],
            send_sem=sub_send.at[j],
            recv_sem=sub_recv.at[j],
            device_id=(sub_peer(j), crs),
            device_id_type=MESH,
        )

    @pl.loop(1, n_crs)
    def _(j):
        crs_copy(j, crs).start()

    crs_in[crs] = mine[...]

    @pl.loop(1, n_crs)
    def _(j):
        crs_copy(j, lax.rem(crs + n_crs - j, n_crs)).wait()

    part[...] = jnp.sum(crs_in[...], axis=0)

    @pl.loop(1, n_sub)
    def _(j):
        sub_copy(j, sub).start()

    sub_in[sub] = part[...]

    @pl.loop(1, n_sub)
    def _(j):
        sub_copy(j, lax.rem(sub + n_sub - j, n_sub)).wait()

    out_ref[...] = jnp.sum(sub_in[...], axis=0)


def scalar_call(n_sub, n_crs, first, second):
    vmem = pl.BlockSpec(memory_space=pltpu.VMEM)
    return pl.pallas_call(
        functools.partial(scalar_kernel, n_sub, n_crs),
        out_shape=jax.ShapeDtypeStruct((8, BS), F32),
        in_specs=[vmem] * 2,
        out_specs=vmem,
        scratch_shapes=[
            pltpu.VMEM((8, BS), F32),
            pltpu.VMEM((n_crs, 8, BS), F32),
            pltpu.VMEM((8, BS), F32),
            pltpu.VMEM((n_sub, 8, BS), F32),
            pltpu.SemaphoreType.DMA((n_crs,)),
            pltpu.SemaphoreType.DMA((n_crs,)),
            pltpu.SemaphoreType.DMA((n_sub,)),
            pltpu.SemaphoreType.DMA((n_sub,)),
        ],
        compiler_params=pltpu.CompilerParams(collective_id=1, has_side_effects=True),
    )(first, second)


def solution(mesh):
    n_sub, n_crs = mesh.shape["sub"], mesh.shape["crs"]

    def per_device(
        right_side,
        kappa_sq,
        conduct,
        partners,
        local_factor,
        restrict_weight,
        aggregate,
        owner,
        owner_coarse_row,
        coarse_factor,
    ):
        nodes = right_side.shape[1]
        slots = owner.shape[0]
        first_block = lax.axis_index(("sub", "crs")) * local_factor.shape[0] - HALO
        rest = (
            local_factor,
            coarse_factor,
            restrict_weight.reshape(1, nodes),
            kappa_sq.reshape(1, nodes),
            conduct.reshape(1, nodes),
            aggregate,
            owner.reshape(1, slots),
            owner_coarse_row.reshape(1, slots),
            (partners - first_block).reshape(-1),
        )
        z, q, first = apply_call(n_sub, n_crs, right_side, *rest)
        u, t, second = apply_call(n_sub, n_crs, q, *rest)
        sums = scalar_call(n_sub, n_crs, first, second)
        rz, zq, qu, ut = (sums[i, :SMP] for i in range(4))
        step = rz / zq
        rz_next = step * step * qu - rz
        ratio = rz_next / rz
        grown = 1.0 + ratio
        curvature = grown * grown * zq - 2.0 * grown * step * qu + step * step * ut
        step_next = rz_next / curvature
        near = (step + step_next * grown)[:, None]
        far = (step * step_next)[:, None]
        return near * z - far * u, right_side - near * q + far * t

    return jax.shard_map(
        per_device,
        mesh=mesh,
        in_specs=(
            P(None, ("sub", "crs")),
            P(("sub", "crs")),
            P(("sub", "crs")),
            P(("sub", "crs"), None),
            P(("sub", "crs"), None, None),
            P(("sub", "crs")),
            P(("sub", "crs"), None),
            P(("sub", "crs"), None),
            P(("sub", "crs")),
            P("crs", "sub"),
        ),
        out_specs=(P(None, ("sub", "crs")), P(None, ("sub", "crs"))),
        check_vma=False,
    )
```

time: 1500 us -> 199 us (0.13)
  waiting for transfers between devices: 565 us -> 0 us
  other arithmetic: 384 us -> 14.5 us
  local copies, waits for them, and re-layouts: 228 us -> 6.18 us
  blocking collectives: 203 us -> 0 us
  Pallas kernels: 0 us -> 177 us
  matrix products: 81.3 us -> 0 us
  starting transfers between devices: 19.3 us -> 0 us
    psum x6 -> x0, waiting for transfers between devices: 399 us -> none  [the longest x2 169 us: coarse_level(): halfway = lax.psum(halfway_part, 'sub')]
    scatter-add x4 -> x0, other arithmetic: 249 us -> none  [the longest x2 240 us: coarse_level(): jax.ops.segment_sum(weighted_values.T, node_slot_table, num_segments=slot...]
    psum x3 -> x0, blocking collectives: 203 us -> none  [the longest x2 134 us: norm_sum(): return lax.psum(jnp.sum(residual * precond, axis=1), ('sub', 'crs'))]
    gather x16 -> x0, local copies, waits for them, and re-layouts: 183 us -> none  [the longest x2 110 us: coarse_level(): jnp.take(slot_values, node_slot_table, axis=1)]
    pallas_call x0 -> x3, Pallas kernels: none -> 177 us  [the longest x2 163 us: apply_call(): pl.pallas_call(functools.partial(apply_kernel, n_sub, n_crs), out_shape=(...]
    reduce_scatter x2 -> x0, waiting for transfers between devices: 154 us -> none  [coarse_level(): lax.psum_scatter(dense_part, 'sub', scatter_dimension=1, tiled=True)]
    dot_general x8 -> x0, matrix products: 81.3 us -> none  [the longest x2 39.8 us: precondition(): jnp.einsum('sbm,bnm->sbn', halfway, local_factor, precision=highest)]
    sub x5 -> x1, other arithmetic: 68.1 us -> 0.69 us  [per_device(): partners - first_block]
  transfers between devices with their start and end apart: 16 -> 0, of which waited for: 12 -> 0; matrix products, arithmetic and copies ran while one was open for 7% -> 0% of each run, Pallas kernels for 0% -> 0%
where the time goes in v1:
time: 199 us
  Pallas kernels  177 us (89%)
  other arithmetic  14.5 us (7%)
  local copies, waits for them, and re-layouts  6.18 us (3%)
    pallas_call x2, Pallas kernels, apply_call(): pl.pallas_call(functools.partial(apply_kernel, n_sub, n_crs), out_shape=(...  163 us
    pallas_call x1, Pallas kernels, scalar_call(): pl.pallas_call(functools.partial(scalar_kernel, n_sub, n_crs), out_shape=...  14.5 us
    add x1, other arithmetic, per_device(): return (near * z - far * u, right_side - near * q + far * t)  12.1 us
    unnamed x16, local copies, waits for them, and re-layouts  5.96 us

profile of v1, /device:TPU:1, one launch (start us, length us, event | category | flops | bytes accessed | tf_op | source)
XLA Modules:
  0.0 198.6 jit_solution(6732268032560542028)
XLA Ops:
  0.6 0.7 broadcast_subtract_fusion
  1.3 0.1 copy.12
  1.4 0.1 reshape.93.partner_ref
  1.5 0.0 copy-start
  1.6 0.8 copy-done
  2.4 0.0 copy-start.1
  2.4 0.8 copy-done.1
  3.2 0.0 copy-start.2
  3.2 0.8 copy-done.2
  4.1 0.0 copy-start.3
  4.1 0.8 copy-done.3
  4.9 0.0 copy-start.6
  4.9 0.7 copy-done.6
  5.6 0.0 copy-start.7
  5.6 0.7 copy-done.7
  6.3 83.5 %shard_map.113 = (f32[64,16384]{1,0:T(8,128)}, f32[64,16384]{1,0:T(8,128)}, f32[2,64,128]{2,1,0:T(8,128)S(1)}) custom-call(f32[64,16384]{1,0:T(8,128)} %src_hbm.1, f32[128,128,128]{2,1,0:T(8,128)} %factor_hbm.3, f32[1024,512]{1,0:T(8,128)} %coarse_hbm.3, f32[1,16384]{1,0:T(1,128)S(1)} %bitcast.45, f32[1,16384]{1,0:T(1,128)S(1)} %bitcast.47, ...), custom_call_target="tpu_custom_call" | custom-call | tf_op jit(solution)/shard_map/pallas_call | solution.py:444
  89.7 0.0 copy-start.4
  89.8 0.6 copy-done.4
  90.4 79.3 %shard_map.114 = (f32[64,16384]{1,0:T(8,128)}, f32[64,16384]{1,0:T(8,128)}, f32[2,64,128]{2,1,0:T(8,128)S(1)}) custom-call(f32[64,16384]{1,0:T(8,128)} %get-tuple-element.9.src_hbm, f32[128,128,128]{2,1,0:T(8,128)} %factor_hbm.3, f32[1024,512]{1,0:T(8,128)} %coarse_hbm.3, f32[1,16384]{1,0:T(1,128)S(1)} %bitcast.46, f32[1,16384]{1,0:T(1,128)S(1)} %bitcast.48, ...), custom_call_target="tpu_custom_call" | custom-call | tf_op jit(solution)/shard_map/pallas_call | solution.py:444
  169.7 0.0 copy-start.5
  169.7 0.6 copy-done.5
  170.3 14.5 %shard_map.115 = f32[8,128]{1,0:T(8,128)} custom-call(f32[2,64,128]{2,1,0:T(8,128)} %copy-done.4, f32[2,64,128]{2,1,0:T(8,128)} %copy-done.5), custom_call_target="tpu_custom_call" | custom-call | tf_op jit(solution)/shard_map/pallas_call | solution.py:574
  184.8 0.8 fusion.4
  185.6 0.8 multiply_add_fusion.1
  186.4 12.1 %multiply_add_fusion = (f32[64,16384]{1,0:T(8,128)}, f32[64,16384]{1,0:T(8,128)}) fusion(f32[64,16384]{1,0:T(8,128)} %get-tuple-element.13, f32[64,16384]{1,0:T(8,128)} %src_hbm.1, f32[64,16384]{1,0:T(8,128)} %get-tuple-element.9.src_hbm, f32[64]{0:T(128)S(1)} %mul.146, f32[64]{0:T(128)S(1)} %get-tuple-element.14, f32[64,16384]{1,0:T(8,128)} %get-tuple-element.12, ...), kind=kLoop, calls=%fused_computation | loop fusion | flops 7340032 | bytes 29360640 | tf_op jit(solution)/shard_map/add | solution.py:634
  (1 shorter events, 0.0 us)
Async XLA Ops:
  1.5 0.8 copy-start
  2.4 0.8 copy-start.1
  3.2 0.8 copy-start.2
  4.1 0.8 copy-start.3
  4.9 0.7 copy-start.6
  5.6 0.7 copy-start.7
  89.7 0.6 copy-start.4
  169.7 0.6 copy-start.5

commit v2 on v1

v2 whole, which is shorter than its diff:
```python
import functools

import jax
import jax.numpy as jnp
from jax import lax
from jax.experimental import pallas as pl
from jax.experimental.pallas import tpu as pltpu
from jax.sharding import PartitionSpec as P

MESH = pl.DeviceIdType.MESH
F32 = jnp.float32
BF16 = jnp.bfloat16
HALO = 7
BS = 128
SMP = 64
LIMIT = 128
VMEM_LIMIT = 40


def split(x):
    high = x.astype(BF16)
    return high, (x - high.astype(F32)).astype(BF16)


def dot(a, b):
    return lax.dot_general(a, b, (((1,), (0,)), ((), ())), preferred_element_type=F32)


def dot_t(a, b):
    return lax.dot_general(a, b, (((1,), (1,)), ((), ())), preferred_element_type=F32)


def stacked(x):
    return jnp.concatenate(split(x), axis=0)


def folded(y):
    half = y.shape[0] // 2
    return y[:half] + y[half:]


def one_hot(mask):
    return jnp.where(mask, 1.0, 0.0).astype(BF16)


def apply_kernel(
    n_sub,
    n_crs,
    src_hbm,
    factor_hbm,
    coarse_hbm,
    weight_hbm,
    kappa_hbm,
    cond_hbm,
    slot_hbm,
    owner_hbm,
    row_hbm,
    partner_ref,
    image_one,
    image_two,
    ext_one,
    ext_two,
    weight_ref,
    kappa_ref,
    slot_ref,
    owner_ref,
    row_ref,
    coarse_high,
    coarse_low,
    src_v,
    factor_v,
    coarse_v,
    cond_v,
    acc_v,
    place_v,
    scatter_v,
    index_send,
    index_recv,
    slot_send,
    slot_recv,
    back_send,
    back_recv,
    cpart,
    crecv,
    cfull,
    ipart,
    irecv,
    ifull,
    lpart,
    lrecv,
    lfull,
    slot_v,
    rates_v,
    dots_ref,
    sums_mine,
    sums_crs,
    sums_part,
    sums_sub,
    load_sem,
    sub_send,
    sub_recv,
    crs_send,
    crs_recv,
    halo_send,
    halo_recv,
):
    sub = lax.axis_index("sub")
    crs = lax.axis_index("crs")
    me = sub * n_crs + crs
    total = n_sub * n_crs
    right = lax.rem(me + 1, total)
    left = lax.rem(me + total - 1, total)
    nodes = src_v.shape[1]
    blocks = nodes // BS
    slots = owner_ref.shape[1]
    halo = HALO * BS

    def sub_peer(j):
        return lax.rem(sub + j, n_sub)

    def sub_from(j):
        return lax.rem(sub + n_sub - j, n_sub)

    def crs_peer(j):
        return lax.rem(crs + j, n_crs)

    def crs_from(j):
        return lax.rem(crs + n_crs - j, n_crs)

    def at_device(d):
        return (d // n_crs, lax.rem(d, n_crs))

    def sub_copy(phase, j, source, target):
        return pltpu.make_async_remote_copy(
            src_ref=source,
            dst_ref=target,
            send_sem=sub_send.at[phase, j],
            recv_sem=sub_recv.at[phase, j],
            device_id=(sub_peer(j), crs),
            device_id_type=MESH,
        )

    def crs_copy(phase, j, source, target):
        return pltpu.make_async_remote_copy(
            src_ref=source,
            dst_ref=target,
            send_sem=crs_send.at[phase, j],
            recv_sem=crs_recv.at[phase, j],
            device_id=(sub, crs_peer(j)),
            device_id_type=MESH,
        )

    def lanes(ref, i):
        return ref.at[:, pl.ds(pl.multiple_of(i * LIMIT, LIMIT), LIMIT)]

    def start_all(count, copy):
        @pl.loop(1, count)
        def _(j):
            copy(j).start()

    def wait_all(count, copy):
        @pl.loop(1, count)
        def _(j):
            copy(j).wait()

    loads = [
        pltpu.make_async_copy(src_hbm, src_v, load_sem.at[0]),
        pltpu.make_async_copy(factor_hbm, factor_v, load_sem.at[1]),
        pltpu.make_async_copy(coarse_hbm, coarse_v, load_sem.at[2]),
        pltpu.make_async_copy(weight_hbm, weight_ref, load_sem.at[3]),
        pltpu.make_async_copy(slot_hbm, slot_ref, load_sem.at[4]),
        pltpu.make_async_copy(owner_hbm, owner_ref, load_sem.at[5]),
        pltpu.make_async_copy(row_hbm, row_ref, load_sem.at[6]),
        pltpu.make_async_copy(cond_hbm, cond_v.at[:, pl.ds(halo, nodes)], load_sem.at[7]),
        pltpu.make_async_copy(kappa_hbm, kappa_ref, load_sem.at[8]),
    ]
    for i in (5, 6, 7, 3, 4, 0, 8, 1, 2):
        loads[i].start()

    barrier = pltpu.get_barrier_semaphore()

    @pl.loop(1, n_sub)
    def _(j):
        pl.semaphore_signal(barrier, inc=1, device_id=(sub_peer(j), crs), device_id_type=MESH)

    @pl.loop(1, n_crs)
    def _(j):
        pl.semaphore_signal(barrier, inc=1, device_id=(sub, crs_peer(j)), device_id_type=MESH)

    pl.semaphore_signal(barrier, inc=1, device_id=at_device(left), device_id_type=MESH)
    pl.semaphore_signal(barrier, inc=1, device_id=at_device(right), device_id_type=MESH)

    loads[5].wait()
    loads[6].wait()
    owner_row = owner_ref[...]
    group = lax.broadcasted_iota(jnp.int32, (n_sub, slots), 0)
    members = jnp.where(owner_row == group, 1.0, 0.0)
    before = one_hot(
        lax.broadcasted_iota(jnp.int32, (slots, slots), 0)
        < lax.broadcasted_iota(jnp.int32, (slots, slots), 1)
    )
    ahead = dot(members.astype(BF16), before)
    rank = jnp.sum(members * ahead, axis=0, keepdims=True)
    place = owner_row * LIMIT + rank.astype(jnp.int32)
    row_one = stacked(jnp.broadcast_to((row_ref[...] + 1).astype(F32), (8, slots)))

    @pl.loop(0, n_sub)
    def _(i):
        start = pl.multiple_of(i * LIMIT, LIMIT)
        hot = one_hot(lax.broadcasted_iota(jnp.int32, (LIMIT, slots), 0) + start == place)
        place_v[pl.ds(start, LIMIT), :] = hot
        index_send[i] = folded(dot_t(row_one, hot)) - 1.0

    loads[7].wait()
    index_recv[sub] = index_send[sub]

    pl.semaphore_wait(barrier, n_sub + n_crs)

    def index_copy(j):
        return sub_copy(0, j, index_send.at[sub_peer(j)], index_recv.at[sub])

    def index_wait(j):
        return sub_copy(0, j, index_send.at[sub_peer(j)], index_recv.at[sub_from(j)])

    start_all(n_sub, index_copy)

    def halo_copies(buffer, phase):
        up = pltpu.make_async_remote_copy(
            src_ref=buffer.at[:, pl.ds(nodes, halo)],
            dst_ref=buffer.at[:, pl.ds(0, halo)],
            send_sem=halo_send.at[phase],
            recv_sem=halo_recv.at[phase],
            device_id=at_device(right),
            device_id_type=MESH,
        )
        down = pltpu.make_async_remote_copy(
            src_ref=buffer.at[:, pl.ds(halo, halo)],
            dst_ref=buffer.at[:, pl.ds(halo + nodes, halo)],
            send_sem=halo_send.at[phase + 1],
            recv_sem=halo_recv.at[phase + 1],
            device_id=at_device(left),
            device_id_type=MESH,
        )
        return up, down

    cond_copies = halo_copies(cond_v, 0)
    for copy in cond_copies:
        copy.start()

    half_rows = coarse_v.shape[0] // 2
    own = pl.ds(pl.multiple_of(sub * LIMIT, LIMIT), LIMIT)
    chunk = 1024
    chunks = nodes // chunk
    lane = lax.broadcasted_iota(jnp.int32, (1, BS), 1)
    dots_ref[...] = jnp.zeros_like(dots_ref)

    def apply(turn, src_v, ext_v, q_v):
        if turn == 0:
            loads[3].wait()
            loads[4].wait()
            loads[0].wait()
        acc_v[...] = jnp.zeros_like(acc_v)

        wide = 2048

        @pl.loop(0, nodes // wide)
        def _(i):
            span = pl.ds(pl.multiple_of(i * wide, wide), wide)
            weighted = src_v[:, span] * weight_ref[:, span]
            hot = one_hot(lax.broadcasted_iota(jnp.int32, (slots, wide), 0) == slot_ref[:, span])
            acc_v[...] += dot_t(hot, stacked(weighted))

        tiles = stacked(folded(jnp.transpose(acc_v[...])))
        for i in range(0, n_sub, 2):
            slot_send[:, i * LIMIT : (i + 2) * LIMIT] = folded(
                dot_t(tiles, place_v[i * LIMIT : (i + 2) * LIMIT, :])
            )

        def slot_copy(j):
            return sub_copy(5 * turn + 1, j, lanes(slot_send, sub_peer(j)), lanes(slot_recv, sub))

        def slot_wait(j):
            return sub_copy(5 * turn + 1, j, lanes(slot_send, sub_peer(j)), lanes(slot_recv, sub_from(j)))

        start_all(n_sub, slot_copy)
        slot_recv[:, own] = slot_send[:, own]

        def local(first, last):
            @pl.loop(first // 4, last // 4)
            def _(g):
                for k in range(4):
                    b = g * 4 + k
                    at = pl.multiple_of(b * BS, BS)
                    values = stacked(src_v[:, pl.ds(at, BS)])
                    high, low = split(factor_v[b])
                    half = folded(dot(values, high)) + dot(values[:SMP], low)
                    half = stacked(half)
                    ext_v[:, pl.ds(pl.multiple_of(at + halo, BS), BS)] = folded(
                        dot_t(half, high)
                    ) + dot_t(half[:SMP], low)

        if turn == 0:
            loads[1].wait()
        local(0, 32)

        if turn == 0:
            wait_all(n_sub, index_wait)

            @pl.loop(0, n_sub)
            def _(i):
                index = index_recv[i][0:1, :].astype(jnp.int32)
                rows = scatter_v.shape[0]
                span = pl.ds(pl.multiple_of(i * LIMIT, LIMIT), LIMIT)
                scatter_v[:, span] = one_hot(lax.broadcasted_iota(jnp.int32, (rows, LIMIT), 0) == index)

        if turn == 0:
            loads[2].wait()
            step_rows = 128

            @pl.loop(0, coarse_v.shape[0] // step_rows)
            def _(i):
                span = pl.ds(pl.multiple_of(i * step_rows, step_rows), step_rows)
                high, low = split(coarse_v[span, :])
                coarse_high[span, :] = high
                coarse_low[span, :] = low

        wait_all(n_sub, slot_wait)
        coarse_part = folded(dot_t(stacked(slot_recv[...]), scatter_v[...]))
        cpart[...] = coarse_part.reshape(cpart.shape)

        def reduce_sub(phase, part, recv, full, gap):
            def out(j):
                return sub_copy(phase, j, part.at[sub_peer(j)], recv.at[sub])

            def come(j):
                return sub_copy(phase, j, part.at[sub_peer(j)], recv.at[sub_from(j)])

            def share(j):
                return sub_copy(phase + 1, j, full.at[sub], full.at[sub])

            def shared(j):
                return sub_copy(phase + 1, j, full.at[sub], full.at[sub_from(j)])

            start_all(n_sub, out)
            recv[sub] = part[sub]
            local(gap, gap + 16)
            wait_all(n_sub, come)
            full[sub] = jnp.sum(recv[...], axis=0)
            start_all(n_sub, share)
            local(gap + 16, gap + 32)
            wait_all(n_sub, shared)

        def reduce_crs(phase, part, recv, full, gap):
            def out(j):
                return crs_copy(phase, j, part.at[crs_peer(j)], recv.at[crs])

            def come(j):
                return crs_copy(phase, j, part.at[crs_peer(j)], recv.at[crs_from(j)])

            def share(j):
                return crs_copy(phase + 1, j, full.at[crs], full.at[crs])

            def shared(j):
                return crs_copy(phase + 1, j, full.at[crs], full.at[crs_from(j)])

            start_all(n_crs, out)
            recv[crs] = part[crs]
            local(gap, gap + 16)
            wait_all(n_crs, come)
            full[crs] = jnp.sum(recv[...], axis=0)
            start_all(n_crs, share)
            local(gap + 16, gap + 32)
            wait_all(n_crs, shared)

        reduce_crs(4 * turn, cpart, crecv, cfull, 32)
        coarse = stacked(cfull[...].reshape(SMP, -1))
        for h in range(2):
            high = coarse_high[h * half_rows : (h + 1) * half_rows, :]
            low = coarse_low[h * half_rows : (h + 1) * half_rows, :]
            inner = folded(dot_t(coarse, high)) + dot_t(coarse[:SMP], low)
            ipart[h * 8 : (h + 1) * 8] = inner.reshape(8, 8, half_rows)

        reduce_sub(5 * turn + 2, ipart, irecv, ifull, 64)
        lifted = jnp.zeros((SMP, coarse_v.shape[1]), F32)
        for h in range(2):
            high = coarse_high[h * half_rows : (h + 1) * half_rows, :]
            low = coarse_low[h * half_rows : (h + 1) * half_rows, :]
            inner = stacked(ifull[h * 8 : (h + 1) * 8].reshape(SMP, half_rows))
            lifted = lifted + folded(dot(inner, high)) + dot(inner[:SMP], low)
        lpart[...] = lifted.reshape(lpart.shape)

        reduce_crs(4 * turn + 2, lpart, lrecv, lfull, 96)
        lifted = stacked(lfull[...].reshape(SMP, -1))
        for i in range(0, n_sub, 2):
            back_send[:, i * LIMIT : (i + 2) * LIMIT] = folded(
                dot(lifted, scatter_v[:, i * LIMIT : (i + 2) * LIMIT])
            )

        def back_copy(j):
            return sub_copy(5 * turn + 4, j, lanes(back_send, sub_peer(j)), lanes(back_recv, sub))

        def back_wait(j):
            return sub_copy(5 * turn + 4, j, lanes(back_send, sub_peer(j)), lanes(back_recv, sub_from(j)))

        start_all(n_sub, back_copy)
        back_recv[:, own] = back_send[:, own]
        if turn == 0:
            for copy in cond_copies:
                copy.wait()
            loads[8].wait()

            @pl.loop(0, blocks)
            def _(b):
                at = pl.multiple_of(b * BS, BS)
                cond = cond_v[:, pl.ds(pl.multiple_of(at + halo, BS), BS)]
                up = jnp.where(lane < BS - 1, 0.5 * (cond + pltpu.roll(cond, BS - 1, 1)), 0.0)
                down = jnp.where(lane > 0, 0.5 * (cond + pltpu.roll(cond, 1, 1)), 0.0)
                whole = kappa_ref[:, pl.ds(at, BS)] + up + down
                for k in range(4):
                    other = pl.ds(partner_ref[k * blocks + b] * BS, BS)
                    weight = 0.5 * (cond + cond_v[:, other])
                    rates_v[b, k : k + 1] = weight
                    whole = whole + weight
                rates_v[b, 4:5] = whole
                rates_v[b, 5:6] = up
                rates_v[b, 6:7] = down

        wait_all(n_sub, back_wait)
        slot_v[...] = stacked(folded(dot(stacked(back_recv[...]), place_v[...])))

        def lift(i):
            at = pl.multiple_of(i * chunk, chunk)
            span = pl.ds(at, chunk)
            hot = one_hot(lax.broadcasted_iota(jnp.int32, (slots, chunk), 0) == slot_ref[:, span])
            inside = pl.ds(pl.multiple_of(at + halo, BS), chunk)
            z = ext_v[:, inside] + weight_ref[:, span] * folded(dot(slot_v[...], hot))
            ext_v[:, inside] = z
            product = z * src_v[:, span]
            total = product[:, :BS]
            for k in range(1, chunk // BS):
                total = total + product[:, k * BS : (k + 1) * BS]
            dots_ref[2 * turn] += total

        @pl.loop(0, 2)
        def _(i):
            lift(i * (chunks - 1))

        halo_now = halo_copies(ext_v, 2 + 2 * turn)
        for copy in halo_now:
            copy.start()

        @pl.loop(1, chunks - 1)
        def _(i):
            lift(i)

        for copy in halo_now:
            copy.wait()

        per_turn = 4

        def operator(g, total):
            images = []
            for i in range(per_turn):
                b = g * per_turn + i
                v = ext_v[:, pl.ds(pl.multiple_of(b * BS + halo, BS), BS)]
                rates = rates_v[b]
                image = rates[4:5] * v
                image = image - rates[5:6] * pltpu.roll(v, BS - 1, 1)
                image = image - rates[6:7] * pltpu.roll(v, 1, 1)
                for k in range(4):
                    other = pl.ds(partner_ref[k * blocks + b] * BS, BS)
                    image = image - rates[k : k + 1] * ext_v[:, other]
                images.append(image)
                total = total + v * image
            for i in range(per_turn):
                at = pl.multiple_of((g * per_turn + i) * BS, BS)
                q_v[:, pl.ds(at, BS)] = images[i]
            return total

        dots_ref[2 * turn + 1] = lax.fori_loop(
            0, blocks // per_turn, operator, jnp.zeros((SMP, BS), F32)
        )

    apply(0, src_v, ext_one, image_one)
    apply(1, image_one, ext_two, image_two)

    kind = lax.broadcasted_iota(jnp.int32, (8, BS), 0)
    packed = jnp.zeros((8, BS), F32)
    ones = jnp.ones((8, BS), F32)
    for i in range(4):
        sums = lax.dot_general(
            ones,
            jnp.concatenate([dots_ref[i], jnp.zeros((BS - SMP, BS), F32)], axis=0),
            (((1,), (1,)), ((), ())),
            precision=lax.Precision.HIGHEST,
            preferred_element_type=F32,
        )
        packed = jnp.where(kind == i, sums, packed)
    sums_mine[...] = packed

    def sums_out(j):
        return crs_copy(8, j, sums_mine, sums_crs.at[crs])

    def sums_come(j):
        return crs_copy(8, j, sums_mine, sums_crs.at[crs_from(j)])

    def part_out(j):
        return sub_copy(10, j, sums_part, sums_sub.at[sub])

    def part_come(j):
        return sub_copy(10, j, sums_part, sums_sub.at[sub_from(j)])

    start_all(n_crs, sums_out)
    sums_crs[crs] = sums_mine[...]
    wait_all(n_crs, sums_come)
    sums_part[...] = jnp.sum(sums_crs[...], axis=0)
    start_all(n_sub, part_out)
    sums_sub[sub] = sums_part[...]
    wait_all(n_sub, part_come)
    sums = jnp.sum(sums_sub[...], axis=0)
    rz, zq, qu, ut = (sums[i : i + 1] for i in range(4))
    step = rz / zq
    rz_next = step * step * qu - rz
    ratio = rz_next / rz
    grown = 1.0 + ratio
    curvature = grown * grown * zq - 2.0 * grown * step * qu + step * step * ut
    step_next = rz_next / curvature
    near = jnp.transpose(jnp.broadcast_to(step + step_next * grown, (BS, BS)))[:SMP]
    far = jnp.transpose(jnp.broadcast_to(step * step_next, (BS, BS)))[:SMP]

    @pl.loop(0, blocks // 2)
    def _(g):
        for k in range(2):
            at = pl.multiple_of((g * 2 + k) * BS, BS)
            span = pl.ds(at, BS)
            inside = pl.ds(pl.multiple_of(at + halo, BS), BS)
            residual = src_v[:, span] - near * image_one[:, span] + far * image_two[:, span]
            image_one[:, span] = near * ext_one[:, inside] - far * ext_two[:, inside]
            image_two[:, span] = residual


def apply_call(n_sub, n_crs, src, factor, coarse_factor, weight, kappa, cond, slot, owner, row, partner):
    nodes = src.shape[1]
    blocks = factor.shape[0]
    slots = owner.shape[1]
    rows, cols = coarse_factor.shape
    halo = HALO * BS
    vmem = pl.BlockSpec(memory_space=pltpu.VMEM)
    anywhere = pl.BlockSpec(memory_space=pltpu.HBM)
    wide = n_sub * LIMIT
    field = jax.ShapeDtypeStruct(src.shape, F32)
    return pl.pallas_call(
        functools.partial(apply_kernel, n_sub, n_crs),
        out_shape=(field, field),
        in_specs=[anywhere] * 9 + [pl.BlockSpec(memory_space=pltpu.SMEM)],
        out_specs=(vmem,) * 2,
        scratch_shapes=[
            pltpu.VMEM((SMP, nodes + 2 * halo), F32),
            pltpu.VMEM((SMP, nodes + 2 * halo), F32),
            pltpu.VMEM((1, nodes), F32),
            pltpu.VMEM((1, nodes), F32),
            pltpu.VMEM((1, nodes), jnp.int32),
            pltpu.VMEM((1, slots), jnp.int32),
            pltpu.VMEM((1, slots), jnp.int32),
            pltpu.VMEM((rows, cols), BF16),
            pltpu.VMEM((rows, cols), BF16),
            pltpu.VMEM((SMP, nodes), F32),
            pltpu.VMEM((blocks, BS, BS), F32),
            pltpu.VMEM((rows, cols), F32),
            pltpu.VMEM((1, nodes + 2 * halo), F32),
            pltpu.VMEM((slots, 2 * SMP), F32),
            pltpu.VMEM((wide, slots), BF16),
            pltpu.VMEM((cols, wide), BF16),
            pltpu.VMEM((n_sub, 8, LIMIT), F32),
            pltpu.VMEM((n_sub, 8, LIMIT), F32),
            pltpu.VMEM((SMP, wide), F32),
            pltpu.VMEM((SMP, wide), F32),
            pltpu.VMEM((SMP, wide), F32),
            pltpu.VMEM((SMP, wide), F32),
            pltpu.VMEM((n_crs, 8, cols), F32),
            pltpu.VMEM((n_crs, 8, cols), F32),
            pltpu.VMEM((n_crs, 8, cols), F32),
            pltpu.VMEM((n_sub, 8, rows // 2), F32),
            pltpu.VMEM((n_sub, 8, rows // 2), F32),
            pltpu.VMEM((n_sub, 8, rows // 2), F32),
            pltpu.VMEM((n_crs, 8, cols), F32),
            pltpu.VMEM((n_crs, 8, cols), F32),
            pltpu.VMEM((n_crs, 8, cols), F32),
            pltpu.VMEM((2 * SMP, slots), BF16),
            pltpu.VMEM((blocks, 8, BS), F32),
            pltpu.VMEM((4, SMP, BS), F32),
            pltpu.VMEM((8, BS), F32),
            pltpu.VMEM((n_crs, 8, BS), F32),
            pltpu.VMEM((8, BS), F32),
            pltpu.VMEM((n_sub, 8, BS), F32),
            pltpu.SemaphoreType.DMA((9,)),
            pltpu.SemaphoreType.DMA((11, n_sub)),
            pltpu.SemaphoreType.DMA((11, n_sub)),
            pltpu.SemaphoreType.DMA((9, n_crs)),
            pltpu.SemaphoreType.DMA((9, n_crs)),
            pltpu.SemaphoreType.DMA((6,)),
            pltpu.SemaphoreType.DMA((6,)),
        ],
        compiler_params=pltpu.CompilerParams(
            collective_id=0, has_side_effects=True, vmem_limit_bytes=VMEM_LIMIT * 1024 * 1024
        ),
    )(src, factor, coarse_factor, weight, kappa, cond, slot, owner, row, partner)


def solution(mesh):
    n_sub, n_crs = mesh.shape["sub"], mesh.shape["crs"]

    def per_device(
        right_side,
        kappa_sq,
        conduct,
        partners,
        local_factor,
        restrict_weight,
        aggregate,
        owner,
        owner_coarse_row,
        coarse_factor,
    ):
        nodes = right_side.shape[1]
        slots = owner.shape[0]
        first_block = lax.axis_index(("sub", "crs")) * local_factor.shape[0] - HALO
        rest = (
            local_factor,
            coarse_factor,
            restrict_weight.reshape(1, nodes),
            kappa_sq.reshape(1, nodes),
            conduct.reshape(1, nodes),
            aggregate,
            owner.reshape(1, slots),
            owner_coarse_row.reshape(1, slots),
            (partners.T - first_block).reshape(-1),
        )
        return apply_call(n_sub, n_crs, right_side, *rest)

    return jax.shard_map(
        per_device,
        mesh=mesh,
        in_specs=(
            P(None, ("sub", "crs")),
            P(("sub", "crs")),
            P(("sub", "crs")),
            P(("sub", "crs"), None),
            P(("sub", "crs"), None, None),
            P(("sub", "crs")),
            P(("sub", "crs"), None),
            P(("sub", "crs"), None),
            P(("sub", "crs")),
            P("crs", "sub"),
        ),
        out_specs=(P(None, ("sub", "crs")), P(None, ("sub", "crs"))),
        check_vma=False,
    )
```

time: 199 us -> 173 us (0.87)
  Pallas kernels: 177 us -> 161 us
  other arithmetic: 14.5 us -> 0.69 us
  local copies, waits for them, and re-layouts: 6.18 us -> 10.3 us
    pallas_call x1 -> x0, Pallas kernels: 14.5 us -> none  [scalar_call(): pl.pallas_call(functools.partial(scalar_kernel, n_sub, n_crs), out_shape=...]
    add x3 -> x0, other arithmetic: 13.8 us -> none  [the longest x1 12.1 us: per_device(): return (near * z - far * u, right_side - near * q + far * t)]
    unnamed x16, local copies, waits for them, and re-layouts: 5.96 us -> 10.3 us
    pallas_call x2 -> x1, Pallas kernels: 163 us -> 161 us  [apply_call(): pl.pallas_call(functools.partial(apply_kernel, n_sub, n_crs), out_shape=(...]
where the time goes in v2:
time: 173 us; the launch traced here: 172 us
  Pallas kernels  161 us (93%)
  local copies, waits for them, and re-layouts  10.3 us (6%)
    pallas_call x1, Pallas kernels, apply_call(): pl.pallas_call(functools.partial(apply_kernel, n_sub, n_crs), out_shape=(...  161 us
    unnamed x16, local copies, waits for them, and re-layouts  10.3 us

profile of v2, /device:TPU:1, one launch (start us, length us, event | category | flops | bytes accessed | tf_op | source)
XLA Modules:
  0.0 172.4 jit_solution(9159185995648439223)
XLA Ops:
  0.6 0.7 subtract_bitcast_fusion.partner_ref
  1.3 0.0 copy-start
  1.3 1.6 copy-done
  2.9 0.0 copy-start.1
  2.9 0.8 copy-done.1
  3.8 0.0 copy-start.2
  3.8 0.8 copy-done.2
  4.6 0.0 copy-start.3
  4.6 0.8 copy-done.3
  5.4 0.0 copy-start.4
  5.4 0.8 copy-done.4
  6.3 0.0 copy-start.5
  6.3 0.7 copy-done.5
  7.0 0.0 copy-start.6
  7.0 0.7 copy-done.6
  7.6 160.7 %shard_map.113 = (f32[64,16384]{1,0:T(8,128)S(1)}, f32[64,16384]{1,0:T(8,128)S(1)}) custom-call(f32[64,16384]{1,0:T(8,128)} %src_hbm.1, f32[128,128,128]{2,1,0:T(8,128)} %factor_hbm.1, f32[1024,512]{1,0:T(8,128)S(1)} %copy-done, f32[1,16384]{1,0:T(1,128)S(1)} %bitcast.9, f32[1,16384]{1,0:T(1,128)S(1)} %bitcast.10, f32[1,16384]{1,0:T(1,128)S(1)} %bitcast.11, ...), custom_call_target="tpu_custom_call" | custom-call | tf_op jit(solution)/shard_map/pallas_call | solution.py:552
  168.4 2.0 %copy.14 = f32[64,16384]{1,0:T(8,128)} copy(f32[64,16384]{1,0:T(8,128)S(1)} %get-tuple-element.4) | data formatting | bytes 8388608
  170.4 2.0 %copy.15 = f32[64,16384]{1,0:T(8,128)} copy(f32[64,16384]{1,0:T(8,128)S(1)} %get-tuple-element.5) | data formatting | bytes 8388608
Async XLA Ops:
  1.3 1.6 copy-start
  2.9 0.8 copy-start.1
  3.8 0.8 copy-start.2
  4.6 0.8 copy-start.3
  5.4 0.8 copy-start.4
  6.3 0.7 copy-start.5
  7.0 0.7 copy-start.6

commit v3 on v2

--- a/solution.py
+++ b/solution.py
@@ -14,6 +14,8 @@
 BS = 128
 SMP = 64
 LIMIT = 128
+RING = 4
+CORES = 2
 VMEM_LIMIT = 40
 
 
@@ -37,6 +39,16 @@
 def folded(y):
     half = y.shape[0] // 2
     return y[:half] + y[half:]
+
+
+def farthest_first(count, depth):
+    width = count // depth
+
+    def hops(j):
+        outer, inner = j // depth, j % depth
+        return 2 * min(outer, width - outer) + 2 * min(inner, depth - inner) * (depth > CORES)
+
+    return sorted(range(1, count), key=lambda j: (-hops(j), j))
 
 
 def one_hot(mask):
@@ -49,12 +61,9 @@
     src_hbm,
     factor_hbm,
     coarse_hbm,
-    weight_hbm,
-    kappa_hbm,
-    cond_hbm,
+    real_hbm,
     slot_hbm,
-    owner_hbm,
-    row_hbm,
+    name_hbm,
     partner_ref,
     image_one,
     image_two,
@@ -115,17 +124,22 @@
     slots = owner_ref.shape[1]
     halo = HALO * BS
 
+    def shifted(place, j, width, depth, sign):
+        outer = lax.rem(lax.div(place, depth) + width + sign * (j // depth), width)
+        inner = lax.rem(lax.rem(place, depth) + depth + sign * (j % depth), depth)
+        return outer * depth + inner
+
     def sub_peer(j):
-        return lax.rem(sub + j, n_sub)
+        return shifted(sub, j, n_sub // RING, RING, 1)
 
     def sub_from(j):
-        return lax.rem(sub + n_sub - j, n_sub)
+        return shifted(sub, j, n_sub // RING, RING, -1)
 
     def crs_peer(j):
-        return lax.rem(crs + j, n_crs)
+        return shifted(crs, j, n_crs // CORES, CORES, 1)
 
     def crs_from(j):
-        return lax.rem(crs + n_crs - j, n_crs)
+        return shifted(crs, j, n_crs // CORES, CORES, -1)
 
     def at_device(d):
         return (d // n_crs, lax.rem(d, n_crs))
@@ -154,8 +168,7 @@
         return ref.at[:, pl.ds(pl.multiple_of(i * LIMIT, LIMIT), LIMIT)]
 
     def start_all(count, copy):
-        @pl.loop(1, count)
-        def _(j):
+        for j in farthest_first(count, RING if count == n_sub else CORES):
             copy(j).start()
 
     def wait_all(count, copy):
@@ -167,12 +180,16 @@
         pltpu.make_async_copy(src_hbm, src_v, load_sem.at[0]),
         pltpu.make_async_copy(factor_hbm, factor_v, load_sem.at[1]),
         pltpu.make_async_copy(coarse_hbm, coarse_v, load_sem.at[2]),
-        pltpu.make_async_copy(weight_hbm, weight_ref, load_sem.at[3]),
+        pltpu.make_async_copy(real_hbm.at[:, pl.ds(0, nodes)], weight_ref, load_sem.at[3]),
         pltpu.make_async_copy(slot_hbm, slot_ref, load_sem.at[4]),
-        pltpu.make_async_copy(owner_hbm, owner_ref, load_sem.at[5]),
-        pltpu.make_async_copy(row_hbm, row_ref, load_sem.at[6]),
-        pltpu.make_async_copy(cond_hbm, cond_v.at[:, pl.ds(halo, nodes)], load_sem.at[7]),
-        pltpu.make_async_copy(kappa_hbm, kappa_ref, load_sem.at[8]),
+        pltpu.make_async_copy(name_hbm.at[:, pl.ds(0, slots)], owner_ref, load_sem.at[5]),
+        pltpu.make_async_copy(name_hbm.at[:, pl.ds(slots, slots)], row_ref, load_sem.at[6]),
+        pltpu.make_async_copy(
+            real_hbm.at[:, pl.ds(2 * nodes, nodes)],
+            cond_v.at[:, pl.ds(halo, nodes)],
+            load_sem.at[7],
+        ),
+        pltpu.make_async_copy(real_hbm.at[:, pl.ds(nodes, nodes)], kappa_ref, load_sem.at[8]),
     ]
     for i in (5, 6, 7, 3, 4, 0, 8, 1, 2):
         loads[i].start()
@@ -204,12 +221,13 @@
     place = owner_row * LIMIT + rank.astype(jnp.int32)
     row_one = stacked(jnp.broadcast_to((row_ref[...] + 1).astype(F32), (8, slots)))
 
-    @pl.loop(0, n_sub)
-    def _(i):
-        start = pl.multiple_of(i * LIMIT, LIMIT)
-        hot = one_hot(lax.broadcasted_iota(jnp.int32, (LIMIT, slots), 0) + start == place)
-        place_v[pl.ds(start, LIMIT), :] = hot
-        index_send[i] = folded(dot_t(row_one, hot)) - 1.0
+    for i in range(0, n_sub, 4):
+        start = i * LIMIT
+        hot = one_hot(lax.broadcasted_iota(jnp.int32, (4 * LIMIT, slots), 0) + start == place)
+        place_v[start : start + 4 * LIMIT, :] = hot
+        index = folded(dot_t(row_one, hot)) - 1.0
+        for k in range(4):
+            index_send[i + k] = index[:, k * LIMIT : (k + 1) * LIMIT]
 
     loads[7].wait()
     index_recv[sub] = index_send[sub]
@@ -539,10 +557,10 @@
             image_two[:, span] = residual
 
 
-def apply_call(n_sub, n_crs, src, factor, coarse_factor, weight, kappa, cond, slot, owner, row, partner):
+def apply_call(n_sub, n_crs, src, factor, coarse_factor, real, slot, name, partner):
     nodes = src.shape[1]
     blocks = factor.shape[0]
-    slots = owner.shape[1]
+    slots = name.shape[1] // 2
     rows, cols = coarse_factor.shape
     halo = HALO * BS
     vmem = pl.BlockSpec(memory_space=pltpu.VMEM)
@@ -552,7 +570,7 @@
     return pl.pallas_call(
         functools.partial(apply_kernel, n_sub, n_crs),
         out_shape=(field, field),
-        in_specs=[anywhere] * 9 + [pl.BlockSpec(memory_space=pltpu.SMEM)],
+        in_specs=[anywhere] * 6 + [pl.BlockSpec(memory_space=pltpu.SMEM)],
         out_specs=(vmem,) * 2,
         scratch_shapes=[
             pltpu.VMEM((SMP, nodes + 2 * halo), F32),
@@ -604,7 +622,7 @@
         compiler_params=pltpu.CompilerParams(
             collective_id=0, has_side_effects=True, vmem_limit_bytes=VMEM_LIMIT * 1024 * 1024
         ),
-    )(src, factor, coarse_factor, weight, kappa, cond, slot, owner, row, partner)
+    )(src, factor, coarse_factor, real, slot, name, partner)
 
 
 def solution(mesh):
@@ -628,12 +646,9 @@
         rest = (
             local_factor,
             coarse_factor,
-            restrict_weight.reshape(1, nodes),
-            kappa_sq.reshape(1, nodes),
-            conduct.reshape(1, nodes),
+            jnp.concatenate([restrict_weight, kappa_sq, conduct]).reshape(1, 3 * nodes),
             aggregate,
-            owner.reshape(1, slots),
-            owner_coarse_row.reshape(1, slots),
+            jnp.concatenate([owner.reshape(slots), owner_coarse_row]).reshape(1, 2 * slots),
             (partners.T - first_block).reshape(-1),
         )
         return apply_call(n_sub, n_crs, right_side, *rest)

time: 173 us -> 164 us (0.948)
  Pallas kernels: 161 us -> 154 us
  local copies, waits for them, and re-layouts: 10.3 us -> 6.45 us
    pallas_call x1, Pallas kernels: 161 us -> 154 us  [apply_call(): pl.pallas_call(functools.partial(apply_kernel, n_sub, n_crs), out_shape=(...]
    unnamed x16 -> x6, local copies, waits for them, and re-layouts: 10.3 us -> 6.45 us
where the time goes in v3:
time: 164 us
  Pallas kernels  154 us (94%)
  local copies, waits for them, and re-layouts  6.45 us (4%)
  other arithmetic  2.31 us (1%)
    pallas_call x1, Pallas kernels, apply_call(): pl.pallas_call(functools.partial(apply_kernel, n_sub, n_crs), out_shape=(...  154 us
    unnamed x6, local copies, waits for them, and re-layouts  6.45 us

profile of v3, /device:TPU:1, one launch (start us, length us, event | category | flops | bytes accessed | tf_op | source)
XLA Modules:
  0.0 163.9 jit_solution(9682874735123728552)
XLA Ops:
  0.6 0.7 subtract_bitcast_fusion.partner_ref
  1.3 0.7 pad_add_fusion
  2.0 0.9 pad_maximum_fusion
  2.9 0.0 copy-start
  3.0 1.6 copy-done
  4.5 0.0 copy-start.1
  4.5 0.8 copy-done.1
  5.4 154.5 %shard_map.113 = (f32[64,16384]{1,0:T(8,128)S(1)}, f32[64,16384]{1,0:T(8,128)S(1)}) custom-call(f32[64,16384]{1,0:T(8,128)} %src_hbm.1, f32[128,128,128]{2,1,0:T(8,128)} %factor_hbm.1, f32[1024,512]{1,0:T(8,128)S(1)} %copy-done, f32[1,49152]{1,0:T(1,128)S(1)} %bitcast.7, s32[1,16384]{1,0:T(1,128)S(1)} %copy-done.1, s32[1,1024]{1,0:T(1,128)S(1)} %bitcast.8, ...), custom_call_target="tpu_custom_call" | custom-call | tf_op jit(solution)/shard_map/pallas_call | solution.py:570
  159.9 2.0 %copy.14 = f32[64,16384]{1,0:T(8,128)} copy(f32[64,16384]{1,0:T(8,128)S(1)} %get-tuple-element.4) | data formatting | bytes 8388608
  161.9 2.0 %copy.15 = f32[64,16384]{1,0:T(8,128)} copy(f32[64,16384]{1,0:T(8,128)S(1)} %get-tuple-element.5) | data formatting | bytes 8388608
Async XLA Ops:
  2.9 1.6 copy-start
  4.5 0.8 copy-start.1

commit v4 on v3

--- a/solution.py
+++ b/solution.py
@@ -221,26 +221,24 @@
     place = owner_row * LIMIT + rank.astype(jnp.int32)
     row_one = stacked(jnp.broadcast_to((row_ref[...] + 1).astype(F32), (8, slots)))
 
-    for i in range(0, n_sub, 4):
-        start = i * LIMIT
-        hot = one_hot(lax.broadcasted_iota(jnp.int32, (4 * LIMIT, slots), 0) + start == place)
-        place_v[start : start + 4 * LIMIT, :] = hot
+    wide = 2048
+    lists = n_sub * wide // nodes
+
+    def list_slots(i):
+        start = pl.multiple_of(i * lists * LIMIT, lists * LIMIT)
+        hot = one_hot(
+            lax.broadcasted_iota(jnp.int32, (lists * LIMIT, slots), 0) + start == place
+        )
+        place_v[pl.ds(start, lists * LIMIT), :] = hot
         index = folded(dot_t(row_one, hot)) - 1.0
-        for k in range(4):
-            index_send[i + k] = index[:, k * LIMIT : (k + 1) * LIMIT]
-
-    loads[7].wait()
-    index_recv[sub] = index_send[sub]
-
-    pl.semaphore_wait(barrier, n_sub + n_crs)
+        for k in range(lists):
+            index_send[i * lists + k] = index[:, k * LIMIT : (k + 1) * LIMIT]
 
     def index_copy(j):
         return sub_copy(0, j, index_send.at[sub_peer(j)], index_recv.at[sub])
 
     def index_wait(j):
         return sub_copy(0, j, index_send.at[sub_peer(j)], index_recv.at[sub_from(j)])
-
-    start_all(n_sub, index_copy)
 
     def halo_copies(buffer, phase):
         up = pltpu.make_async_remote_copy(
@@ -262,8 +260,6 @@
         return up, down
 
     cond_copies = halo_copies(cond_v, 0)
-    for copy in cond_copies:
-        copy.start()
 
     half_rows = coarse_v.shape[0] // 2
     own = pl.ds(pl.multiple_of(sub * LIMIT, LIMIT), LIMIT)
@@ -272,21 +268,29 @@
     lane = lax.broadcasted_iota(jnp.int32, (1, BS), 1)
     dots_ref[...] = jnp.zeros_like(dots_ref)
 
+    def restrict(values, i):
+        span = pl.ds(pl.multiple_of(i * wide, wide), wide)
+        weighted = stacked(values[:, span] * weight_ref[:, span])
+        hot = one_hot(lax.broadcasted_iota(jnp.int32, (slots, wide), 0) == slot_ref[:, span])
+        acc_v[...] += dot_t(hot, weighted)
+
     def apply(turn, src_v, ext_v, q_v):
         if turn == 0:
             loads[3].wait()
             loads[4].wait()
             loads[0].wait()
-        acc_v[...] = jnp.zeros_like(acc_v)
-
-        wide = 2048
-
-        @pl.loop(0, nodes // wide)
-        def _(i):
-            span = pl.ds(pl.multiple_of(i * wide, wide), wide)
-            weighted = src_v[:, span] * weight_ref[:, span]
-            hot = one_hot(lax.broadcasted_iota(jnp.int32, (slots, wide), 0) == slot_ref[:, span])
-            acc_v[...] += dot_t(hot, stacked(weighted))
+        if turn == 0:
+            acc_v[...] = jnp.zeros_like(acc_v)
+
+            @pl.loop(0, nodes // wide)
+            def _(i):
+                restrict(src_v, i)
+                list_slots(i)
+
+            index_recv[sub] = index_send[sub]
+            loads[7].wait()
+            pl.semaphore_wait(barrier, n_sub + n_crs)
+            start_all(n_sub, index_copy)
 
         tiles = stacked(folded(jnp.transpose(acc_v[...])))
         for i in range(0, n_sub, 2):
@@ -301,6 +305,9 @@
             return sub_copy(5 * turn + 1, j, lanes(slot_send, sub_peer(j)), lanes(slot_recv, sub_from(j)))
 
         start_all(n_sub, slot_copy)
+        if turn == 0:
+            for copy in cond_copies:
+                copy.start()
         slot_recv[:, own] = slot_send[:, own]
 
         def local(first, last):
@@ -495,9 +502,25 @@
                 q_v[:, pl.ds(at, BS)] = images[i]
             return total
 
-        dots_ref[2 * turn + 1] = lax.fori_loop(
-            0, blocks // per_turn, operator, jnp.zeros((SMP, BS), F32)
-        )
+        zero = jnp.zeros((SMP, BS), F32)
+        if turn == 0:
+            groups = wide // BS // per_turn
+
+            def operate(i, total):
+                for g in range(groups):
+                    total = operator(i * groups + g, total)
+                return total
+
+            def both(i, total):
+                restrict(q_v, i - 1)
+                return operate(i, total)
+
+            acc_v[...] = jnp.zeros_like(acc_v)
+            first = operate(0, zero)
+            dots_ref[1] = lax.fori_loop(1, nodes // wide, both, first)
+            restrict(q_v, nodes // wide - 1)
+        else:
+            dots_ref[3] = lax.fori_loop(0, blocks // per_turn, operator, zero)
 
     apply(0, src_v, ext_one, image_one)
     apply(1, image_one, ext_two, image_two)

time: 164 us -> 161 us (0.982)
  Pallas kernels: 154 us -> 152 us
    pallas_call x1, Pallas kernels: 154 us -> 152 us  [apply_call(): pl.pallas_call(functools.partial(apply_kernel, n_sub, n_crs), out_shape=(...]
where the time goes in v4:
time: 161 us
  Pallas kernels  152 us (94%)
  local copies, waits for them, and re-layouts  6.45 us (4%)
  other arithmetic  2.31 us (1%)
    pallas_call x1, Pallas kernels, apply_call(): pl.pallas_call(functools.partial(apply_kernel, n_sub, n_crs), out_shape=(...  152 us
    unnamed x6, local copies, waits for them, and re-layouts  6.45 us

profile of v4, /device:TPU:1, one launch (start us, length us, event | category | flops | bytes accessed | tf_op | source)
XLA Modules:
  0.0 161.1 jit_solution(5565196769867619408)
XLA Ops:
  0.6 0.7 subtract_bitcast_fusion.partner_ref
  1.3 0.7 pad_add_fusion
  2.0 0.9 pad_maximum_fusion
  2.9 0.0 copy-start
  3.0 1.6 copy-done
  4.5 0.0 copy-start.1
  4.5 0.8 copy-done.1
  5.4 151.7 %shard_map.113 = (f32[64,16384]{1,0:T(8,128)S(1)}, f32[64,16384]{1,0:T(8,128)S(1)}) custom-call(f32[64,16384]{1,0:T(8,128)} %src_hbm.1, f32[128,128,128]{2,1,0:T(8,128)} %factor_hbm.1, f32[1024,512]{1,0:T(8,128)S(1)} %copy-done, f32[1,49152]{1,0:T(1,128)S(1)} %bitcast.7, s32[1,16384]{1,0:T(1,128)S(1)} %copy-done.1, s32[1,1024]{1,0:T(1,128)S(1)} %bitcast.8, ...), custom_call_target="tpu_custom_call" | custom-call | tf_op jit(solution)/shard_map/pallas_call | solution.py:593
  157.1 2.0 %copy.14 = f32[64,16384]{1,0:T(8,128)} copy(f32[64,16384]{1,0:T(8,128)S(1)} %get-tuple-element.4) | data formatting | bytes 8388608
  159.1 2.0 %copy.15 = f32[64,16384]{1,0:T(8,128)} copy(f32[64,16384]{1,0:T(8,128)S(1)} %get-tuple-element.5) | data formatting | bytes 8388608
Async XLA Ops:
  2.9 1.6 copy-start
  4.5 0.8 copy-start.1

commit v5 on v4

--- a/solution.py
+++ b/solution.py
@@ -62,7 +62,6 @@
     factor_hbm,
     coarse_hbm,
     real_hbm,
-    slot_hbm,
     name_hbm,
     partner_ref,
     image_one,
@@ -181,7 +180,7 @@
         pltpu.make_async_copy(factor_hbm, factor_v, load_sem.at[1]),
         pltpu.make_async_copy(coarse_hbm, coarse_v, load_sem.at[2]),
         pltpu.make_async_copy(real_hbm.at[:, pl.ds(0, nodes)], weight_ref, load_sem.at[3]),
-        pltpu.make_async_copy(slot_hbm, slot_ref, load_sem.at[4]),
+        pltpu.make_async_copy(real_hbm.at[:, pl.ds(3 * nodes, nodes)], slot_ref, load_sem.at[4]),
         pltpu.make_async_copy(name_hbm.at[:, pl.ds(0, slots)], owner_ref, load_sem.at[5]),
         pltpu.make_async_copy(name_hbm.at[:, pl.ds(slots, slots)], row_ref, load_sem.at[6]),
         pltpu.make_async_copy(
@@ -271,7 +270,7 @@
     def restrict(values, i):
         span = pl.ds(pl.multiple_of(i * wide, wide), wide)
         weighted = stacked(values[:, span] * weight_ref[:, span])
-        hot = one_hot(lax.broadcasted_iota(jnp.int32, (slots, wide), 0) == slot_ref[:, span])
+        hot = one_hot(lax.broadcasted_iota(jnp.int32, (slots, wide), 0) == slot_ref[:, span].astype(jnp.int32))
         acc_v[...] += dot_t(hot, weighted)
 
     def apply(turn, src_v, ext_v, q_v):
@@ -456,7 +455,7 @@
         def lift(i):
             at = pl.multiple_of(i * chunk, chunk)
             span = pl.ds(at, chunk)
-            hot = one_hot(lax.broadcasted_iota(jnp.int32, (slots, chunk), 0) == slot_ref[:, span])
+            hot = one_hot(lax.broadcasted_iota(jnp.int32, (slots, chunk), 0) == slot_ref[:, span].astype(jnp.int32))
             inside = pl.ds(pl.multiple_of(at + halo, BS), chunk)
             z = ext_v[:, inside] + weight_ref[:, span] * folded(dot(slot_v[...], hot))
             ext_v[:, inside] = z
@@ -481,7 +480,7 @@
         for copy in halo_now:
             copy.wait()
 
-        per_turn = 4
+        per_turn = 8
 
         def operator(g, total):
             images = []
@@ -580,7 +579,7 @@
             image_two[:, span] = residual
 
 
-def apply_call(n_sub, n_crs, src, factor, coarse_factor, real, slot, name, partner):
+def apply_call(n_sub, n_crs, src, factor, coarse_factor, real, name, partner):
     nodes = src.shape[1]
     blocks = factor.shape[0]
     slots = name.shape[1] // 2
@@ -593,14 +592,14 @@
     return pl.pallas_call(
         functools.partial(apply_kernel, n_sub, n_crs),
         out_shape=(field, field),
-        in_specs=[anywhere] * 6 + [pl.BlockSpec(memory_space=pltpu.SMEM)],
+        in_specs=[anywhere] * 5 + [pl.BlockSpec(memory_space=pltpu.SMEM)],
         out_specs=(vmem,) * 2,
         scratch_shapes=[
             pltpu.VMEM((SMP, nodes + 2 * halo), F32),
             pltpu.VMEM((SMP, nodes + 2 * halo), F32),
             pltpu.VMEM((1, nodes), F32),
             pltpu.VMEM((1, nodes), F32),
-            pltpu.VMEM((1, nodes), jnp.int32),
+            pltpu.VMEM((1, nodes), F32),
             pltpu.VMEM((1, slots), jnp.int32),
             pltpu.VMEM((1, slots), jnp.int32),
             pltpu.VMEM((rows, cols), BF16),
@@ -645,7 +644,7 @@
         compiler_params=pltpu.CompilerParams(
             collective_id=0, has_side_effects=True, vmem_limit_bytes=VMEM_LIMIT * 1024 * 1024
         ),
-    )(src, factor, coarse_factor, real, slot, name, partner)
+    )(src, factor, coarse_factor, real, name, partner)
 
 
 def solution(mesh):
@@ -669,8 +668,9 @@
         rest = (
             local_factor,
             coarse_factor,
-            jnp.concatenate([restrict_weight, kappa_sq, conduct]).reshape(1, 3 * nodes),
-            aggregate,
+            jnp.concatenate(
+                [restrict_weight, kappa_sq, conduct, aggregate[0].astype(F32)]
+            ).reshape(1, 4 * nodes),
             jnp.concatenate([owner.reshape(slots), owner_coarse_row]).reshape(1, 2 * slots),
             (partners.T - first_block).reshape(-1),
         )

time: 161 us -> 160 us (level)
  Pallas kernels: 152 us -> 150 us
    unnamed x6 -> x4, local copies, waits for them, and re-layouts: 6.45 us -> 5.61 us
where the time goes in v5:
time: 160 us
  Pallas kernels  150 us (94%)
  local copies, waits for them, and re-layouts  5.61 us (4%)
  other arithmetic  3.2 us (2%)
    pallas_call x1, Pallas kernels, apply_call(): pl.pallas_call(functools.partial(apply_kernel, n_sub, n_crs), out_shape=(...  150 us
    unnamed x4, local copies, waits for them, and re-layouts  5.61 us

profile of v5, /device:TPU:1, one launch (start us, length us, event | category | flops | bytes accessed | tf_op | source)
XLA Modules:
  0.0 159.8 jit_solution(3112305714350127908)
XLA Ops:
  0.6 0.7 subtract_bitcast_fusion.partner_ref
  1.3 0.7 pad_add_fusion
  2.0 0.9 convert_element_type.6
  2.9 0.9 pad_maximum_fusion
  3.8 0.0 copy-start
  3.9 1.6 copy-done
  5.4 150.4 %shard_map.113 = (f32[64,16384]{1,0:T(8,128)S(1)}, f32[64,16384]{1,0:T(8,128)S(1)}) custom-call(f32[64,16384]{1,0:T(8,128)} %src_hbm.1, f32[128,128,128]{2,1,0:T(8,128)} %factor_hbm.1, f32[1024,512]{1,0:T(8,128)S(1)} %copy-done, f32[1,65536]{1,0:T(1,128)S(1)} %bitcast.8, s32[1,1024]{1,0:T(1,128)S(1)} %bitcast.9, s32[512]{0:T(512)S(1)} %subtract_bitcast_fusion.partner_ref), custom_call_target="tpu_custom_call" | custom-call | tf_op jit(solution)/shard_map/pallas_call | solution.py:592
  155.8 2.0 %copy.14 = f32[64,16384]{1,0:T(8,128)} copy(f32[64,16384]{1,0:T(8,128)S(1)} %get-tuple-element.4) | data formatting | bytes 8388608
  157.8 2.0 %copy.15 = f32[64,16384]{1,0:T(8,128)} copy(f32[64,16384]{1,0:T(8,128)S(1)} %get-tuple-element.5) | data formatting | bytes 8388608
Async XLA Ops:
  3.8 1.6 copy-start

commit v6 on v5

--- a/solution.py
+++ b/solution.py
@@ -325,7 +325,7 @@
 
         if turn == 0:
             loads[1].wait()
-        local(0, 32)
+        local(0, 16)
 
         if turn == 0:
             wait_all(n_sub, index_wait)
@@ -367,11 +367,11 @@
 
             start_all(n_sub, out)
             recv[sub] = part[sub]
-            local(gap, gap + 16)
+            local(gap, gap + 24)
             wait_all(n_sub, come)
             full[sub] = jnp.sum(recv[...], axis=0)
             start_all(n_sub, share)
-            local(gap + 16, gap + 32)
+            local(gap + 24, gap + 48)
             wait_all(n_sub, shared)
 
         def reduce_crs(phase, part, recv, full, gap):
@@ -396,7 +396,7 @@
             local(gap + 16, gap + 32)
             wait_all(n_crs, shared)
 
-        reduce_crs(4 * turn, cpart, crecv, cfull, 32)
+        reduce_crs(4 * turn, cpart, crecv, cfull, 16)
         coarse = stacked(cfull[...].reshape(SMP, -1))
         for h in range(2):
             high = coarse_high[h * half_rows : (h + 1) * half_rows, :]
@@ -404,7 +404,7 @@
             inner = folded(dot_t(coarse, high)) + dot_t(coarse[:SMP], low)
             ipart[h * 8 : (h + 1) * 8] = inner.reshape(8, 8, half_rows)
 
-        reduce_sub(5 * turn + 2, ipart, irecv, ifull, 64)
+        reduce_sub(5 * turn + 2, ipart, irecv, ifull, 48)
         lifted = jnp.zeros((SMP, coarse_v.shape[1]), F32)
         for h in range(2):
             high = coarse_high[h * half_rows : (h + 1) * half_rows, :]

time: 160 us -> 160 us (level)
  no operation moved by 1% of the time
where the time goes in v6:
time: 160 us
  Pallas kernels  150 us (94%)
  local copies, waits for them, and re-layouts  5.61 us (4%)
  other arithmetic  3.2 us (2%)
    pallas_call x1, Pallas kernels, apply_call(): pl.pallas_call(functools.partial(apply_kernel, n_sub, n_crs), out_shape=(...  150 us
    unnamed x4, local copies, waits for them, and re-layouts  5.61 us

profile of v6, /device:TPU:1, one launch (start us, length us, event | category | flops | bytes accessed | tf_op | source)
XLA Modules:
  0.0 159.8 jit_solution(1608062995014227923)
XLA Ops:
  0.6 0.7 subtract_bitcast_fusion.partner_ref
  1.3 0.7 pad_add_fusion
  2.0 0.9 convert_element_type.6
  2.9 0.9 pad_maximum_fusion
  3.8 0.0 copy-start
  3.9 1.6 copy-done
  5.4 150.4 %shard_map.113 = (f32[64,16384]{1,0:T(8,128)S(1)}, f32[64,16384]{1,0:T(8,128)S(1)}) custom-call(f32[64,16384]{1,0:T(8,128)} %src_hbm.1, f32[128,128,128]{2,1,0:T(8,128)} %factor_hbm.1, f32[1024,512]{1,0:T(8,128)S(1)} %copy-done, f32[1,65536]{1,0:T(1,128)S(1)} %bitcast.8, s32[1,1024]{1,0:T(1,128)S(1)} %bitcast.9, s32[512]{0:T(512)S(1)} %subtract_bitcast_fusion.partner_ref), custom_call_target="tpu_custom_call" | custom-call | tf_op jit(solution)/shard_map/pallas_call | solution.py:592
  155.8 2.0 %copy.14 = f32[64,16384]{1,0:T(8,128)} copy(f32[64,16384]{1,0:T(8,128)S(1)} %get-tuple-element.4) | data formatting | bytes 8388608
  157.8 2.0 %copy.15 = f32[64,16384]{1,0:T(8,128)} copy(f32[64,16384]{1,0:T(8,128)S(1)} %get-tuple-element.5) | data formatting | bytes 8388608
Async XLA Ops:
  3.8 1.6 copy-start
